TPU v7x, 512 devices: a whole 4x8x8 slice. The times are simulated.
512 devices in a mesh: section: 8 (over x, core), expert: 64 (over y, z).
Axes of the slice: x: 4, y: 8, z: 8, core: 2. Of those that a mesh axis runs over, the one named last changes fastest.
Arguments:
- grad_codes: bfloat16 [8, 8192, 4096], P('section', 'expert'), may hold values from -127 to 127, as said below
- grad_scales: bfloat16 [8, 8192], P('section', 'expert'), may hold values from 0.0009994507 to 0.0099487305
- routes: int32 [8, 8192, 2], P('section', 'expert'), may hold values from 0 to 15, as said below
- router_logits: float32 [8, 8192, 16], P('section', 'expert'), may hold values from -12 to 310
- expert_outputs: bfloat16 [8, 64, 1536, 1024], P('section', 'expert'), may hold values from -1.1953125 to 1.1953125
Outputs:
- logit_grad: float32 [8, 8192, 16], P('section', 'expert')
Inputs may be any that keep to these rules, and one draw needn't show every extreme that they name: `grad_codes`: integer values. `routes`: each token names two different experts; among the rows of one device no expert is named more than 24 times, and in each section some expert is named exactly 24 times on every device.
All inputs are finite; a program needn't handle non-finite values.
Results may differ from a plain program's by a relative error of at most 0.009.
Values may be sent and summed in bfloat16 or wider, within the bound.
No kernel may reach another device: no remote copies, remote signals or barrier semaphores. Data moves between devices by JAX's collectives and lax.ppermute only.
A program may use at most 64 MiB of HBM per device.

v0:
```python
import jax
import jax.numpy as jnp
from jax import lax
from jax.sharding import PartitionSpec as P


def shifted(x, axis, by):
    devices = lax.axis_size(axis)
    return lax.ppermute(x, axis, [(i, (i + by) % devices) for i in range(devices)])


def owner_rows(saved, source_counts, slot_count):
    offsets = jnp.cumsum(source_counts) - source_counts
    slot_ids = jnp.arange(slot_count, dtype=jnp.int32)
    position = offsets[:, None] + slot_ids[None, :]
    valid = slot_ids[None, :] < source_counts[:, None]
    picked_rows = jnp.take(saved, jnp.minimum(position, saved.shape[0] - 1), axis=0)
    return jnp.where(valid[:, :, None], picked_rows, jnp.zeros_like(picked_rows))


def local(grad_codes, grad_scales, routes, router_logits, expert_outputs):
    quant_codes, scales = shifted((grad_codes[0], grad_scales[0]), "section", -1)
    gradient = (quant_codes.astype(jnp.float32) * scales.astype(jnp.float32)[:, None]).astype(
        jnp.bfloat16
    )
    owners = lax.axis_size("expert")
    tok_rows, width = gradient.shape
    experts = router_logits.shape[2]
    replicas = owners // experts
    quarter = width // replicas
    saved = expert_outputs[0, 0]
    slot_count = saved.shape[0] // owners
    chosen = routes[0]
    expert_ids = jnp.arange(experts, dtype=jnp.int32)
    chosen_hit = (chosen[:, :, None] == expert_ids[None, None, :]).astype(jnp.int32)
    per_token = jnp.sum(chosen_hit, axis=1)
    before = jnp.cumsum(per_token, axis=0) - per_token
    slot_index = jnp.sum(chosen_hit * before[:, None, :], axis=2)
    counts = jnp.sum(per_token, axis=0)
    slot_hit = (
        slot_index[:, :, None] == jnp.arange(slot_count, dtype=jnp.int32)[None, None, :]
    ).astype(jnp.float32)
    selector = jnp.einsum("tce,tck->ekt", chosen_hit.astype(jnp.float32), slot_hit)
    split_rows = gradient.reshape(tok_rows, replicas, quarter)
    packed = jnp.einsum(
        "ekt,trq->erkq",
        selector.astype(jnp.bfloat16),
        split_rows,
        preferred_element_type=jnp.float32,
    )
    packed = packed.astype(jnp.bfloat16).reshape(owners, slot_count, quarter)
    count_column = jnp.repeat(counts, replicas)[:, None]
    arrived, arrived_counts = (
        lax.all_to_all(packed, "expert", split_axis=0, concat_axis=0, tiled=True),
        lax.all_to_all(
            count_column.astype(jnp.bfloat16), "expert", split_axis=0, concat_axis=0, tiled=True
        ),
    )
    source_counts = arrived_counts[:, 0].astype(jnp.int32)
    saved_rows = owner_rows(saved, source_counts, slot_count)
    products = jnp.einsum("jkq,jkq->jk", arrived, saved_rows, preferred_element_type=jnp.float32)
    returned = lax.all_to_all(products, "expert", split_axis=0, concat_axis=0, tiled=True)
    slot_grad = jnp.sum(returned.reshape(experts, replicas, slot_count), axis=1)
    gate_terms = jnp.einsum("ekt,ek->te", selector, slot_grad)
    router_probs = jax.nn.softmax(router_logits[0], axis=-1)
    logit_grad = router_probs * (
        gate_terms - jnp.sum(router_probs * gate_terms, axis=-1, keepdims=True)
    )
    return logit_grad[None]


def solution(mesh):
    placed = (
        P("section", "expert", None),
        P("section", "expert"),
        P("section", "expert", None),
        P("section", "expert", None),
        P("section", "expert", None, None),
    )
    return jax.shard_map(
        local, mesh=mesh, in_specs=placed, out_specs=P("section", "expert", None), check_vma=False
    )
```

profile of v0, /device:TPU:6, one launch (start us, length us, event | category | flops | bytes accessed | tf_op | source)
XLA Modules:
  0.0 165.8 jit_solution(12171971173931711324)
XLA Ops:
  0.0 0.3 collective-permute-start
  0.3 0.7 collective-permute-start.1
  0.9 0.8 copy.27
  1.7 0.3 convert_reduce_fusion.1
  2.0 0.2 reduce_window_sum.18
  2.2 2.4 %convert_reduce_fusion = (s32[16]{0:T(128)S(1)}, s32[128,2]{1,0:T(8,128)S(1)}) fusion(s32[128,2]{1,0:T(8,128)S(1)} %copy.27, s32[128,16]{1,0:T(8,128)S(1)} %sub.32), kind=kLoop, calls=%fused_computation.11 | loop fusion | flops 20208 | bytes 10304 | tf_op jit(solution)/shard_map/reduce_sum | solution.py:39
  4.7 0.7 convert_element_type.80
  5.3 16.6 %all-to-all-start.1 = ((bf16[64,1,1]{2,1,0:T(2,128)(2,1)}), bf16[64,1,1]{2,1,0:T(2,128)(2,1)S(1)}, u32[]{:S(2)}, u32[]{:S(2)}) async-start(bf16[64,1,1]{2,1,0:T(2,128)(2,1)} %convert_element_type.80), calls=%async_computation.1 | async-start | bytes 65536 | tf_op jit(solution)/shard_map/all_to_all | solution.py:55
  21.9 1.8 %fusion.2 = bf16[128,24,16]{1,2,0:T(8,128)(2,1)} fusion(s32[128,2]{1,0:T(8,128)S(1)} %get-tuple-element.6, s32[128,2]{1,0:T(8,128)S(1)} %copy.27), kind=kOutput, calls=%fused_computation.6 | convolution fusion | flops 215040 | bytes 100352 | tf_op jit(solution)/shard_map/tce,tck->ekt/dot_general | solution.py:43
  23.7 1.4 copy.28
  25.2 2.5 %multiply_convert_fusion = bf16[128,4096]{1,0:T(8,128)(2,1)} fusion(bf16[128,4096]{1,0:T(8,128)(2,1)} %collective-permute-done, f32[128]{0:T(128)S(1)} %convert_element_type.65), kind=kLoop, calls=%fused_computation.4 | loop fusion | flops 1572864 | bytes 2097664 | tf_op jit(solution)/shard_map/convert_element_type | solution.py:23
  27.7 2.6 %reshape.158 = bf16[128,4,1024]{2,1,0:T(4,128)(2,1)} reshape(bf16[128,4096]{1,0:T(8,128)(2,1)} %multiply_convert_fusion) | data formatting | bytes 2097152 | tf_op jit(solution)/shard_map/reshape | solution.py:44
  30.4 2.3 %convert_bitcast_fusion = bf16[16,4,24,1024]{3,2,0,1:T(8,128)(2,1)S(1)} fusion(bf16[128,4,1024,1]{2,1,0,3:T(4,128)(2,1)} %bitcast.49, bf16[128,24,16]{0,1,2:T(8,128)(2,1)S(1)} %copy.28), kind=kOutput, calls=%fused_computation.3 | convolution fusion | flops 404226048 | bytes 4292608 | tf_op jit(solution)/shard_map/ekt,trq->erkq/dot_general | solution.py:45
  32.7 2.1 %copy.30 = bf16[16,4,24,1024]{3,2,1,0:T(8,128)(2,1)} copy(bf16[16,4,24,1024]{3,2,0,1:T(8,128)(2,1)S(1)} %convert_bitcast_fusion) | data formatting | bytes 6291456 | tf_op jit(solution)/shard_map/convert_element_type | solution.py:51
  34.9 13.1 %all-to-all-start = ((bf16[64,24,1024]{2,1,0:T(8,128)(2,1)}), bf16[64,24,1024]{2,1,0:T(8,128)(2,1)}, u32[]{:S(2)}, u32[]{:S(2)}) async-start(bf16[64,24,1024]{2,1,0:T(8,128)(2,1)} %bitcast.47), calls=%async_computation | async-start | bytes 6291456 | tf_op jit(solution)/shard_map/all_to_all | solution.py:54
  48.1 0.1 reduce.4
  48.2 1.2 convert_reduce_fusion.2
  49.6 5.9 %gather_fusion = bf16[1536,1024]{1,0:T(8,128)(2,1)} fusion(bf16[1536,1024]{1,0:T(8,128)(2,1)S(1)} %bitcast.46, s32[2048]{0:T(1024)S(1)} %pad_clamp_fusion), kind=kCustom, calls=%fused_computation | custom fusion | bytes 6297600 | tf_op jit(solution)/shard_map/jit(_take)/gather | solution.py:17
  55.6 68.0 %all-to-all-done = bf16[64,24,1024]{2,1,0:T(8,128)(2,1)} async-done(((bf16[64,24,1024]{2,1,0:T(8,128)(2,1)}), bf16[64,24,1024]{2,1,0:T(8,128)(2,1)}, u32[]{:S(2)}, u32[]{:S(2)}) %all-to-all-start) | async-done | bytes 3145760 | tf_op jit(solution)/shard_map/all_to_all | solution.py:54
  123.6 4.3 %fusion = f32[64,24]{1,0:T(8,128)} fusion(bf16[64,24,1024]{2,1,0:T(8,128)(2,1)} %all-to-all-done, bf16[64,24,1024]{2,1,0:T(8,128)(2,1)} %bitcast.48, pred[64,24]{1,0:T(8,128)(4,1)S(1)} %get-tuple-element.8, pred[64,24]{1,0:T(8,128)(4,1)S(1)} %get-tuple-element.7), kind=kLoop, calls=%fused_computation.2 | loop fusion | flops 9435648 | bytes 6300672 | tf_op jit(solution)/shard_map/jkq,jkq->jk/dot_general | solution.py:61
  128.0 25.0 %all-to-all-start.2 = ((f32[64,1,24]{2,1,0:T(1,128)}), f32[64,1,24]{2,1,0:T(1,128)S(1)}, u32[]{:S(2)}, u32[]{:S(2)}) async-start(f32[64,1,24]{2,1,0:T(1,128)} %bitcast.12), calls=%async_computation.2 | async-start | bytes 65536 | tf_op jit(solution)/shard_map/all_to_all | solution.py:62
  153.0 11.9 %all-to-all-done.2 = f32[64,1,24]{2,1,0:T(1,128)S(1)} async-done(((f32[64,1,24]{2,1,0:T(1,128)}), f32[64,1,24]{2,1,0:T(1,128)S(1)}, u32[]{:S(2)}, u32[]{:S(2)}) %all-to-all-start.2) | async-done | bytes 6176 | tf_op jit(solution)/shard_map/all_to_all | solution.py:62
  165.0 0.2 fusion.4
  165.2 0.6 multiply_bitcast_fusion
  (22 shorter events, 0.6 us)
Async XLA Ops:
  0.0 49.6 %copy-start = (bf16[1,1,1536,1024]{3,2,1,0:T(8,128)(2,1)S(1)}, bf16[1,1,1536,1024]{3,2,1,0:T(8,128)(2,1)}, u32[]{:S(2)}) copy-start(bf16[1,1,1536,1024]{3,2,1,0:T(8,128)(2,1)} %param.9) | copy-start | bytes 9437188
  0.0 25.2 %collective-permute-start = (bf16[128,4096]{1,0:T(8,128)(2,1)}, bf16[128,4096]{1,0:T(8,128)(2,1)}, u32[]{:S(2)}, u32[]{:S(2)}) collective-permute-start(bf16[128,4096]{1,0:T(8,128)(2,1)} %bitcast.56), channel_id=1, source_target_pairs={{0,448},{64,0},{128,64},{192,128},{256,192},{320,256},{384,320},{4... | collective-permute-start | bytes 3145736 | tf_op jit(solution)/shard_map/ppermute | solution.py:9
  0.3 24.9 %collective-permute-start.1 = (bf16[128]{0:T(256)(128)(2,1)}, bf16[128]{0:T(256)(128)(2,1)S(1)}, u32[]{:S(2)}, u32[]{:S(2)}) collective-permute-start(bf16[128]{0:T(256)(128)(2,1)} %bitcast.57), channel_id=1, source_target_pairs={{0,448},{64,0},{128,64},{192,128},{256,192},{320,256},{384,320},{4... | collective-permute-start | bytes 776 | tf_op jit(solution)/shard_map/ppermute | solution.py:9
  5.3 29.5 %all-to-all-start.1 = ((bf16[64,1,1]{2,1,0:T(2,128)(2,1)}), bf16[64,1,1]{2,1,0:T(2,128)(2,1)S(1)}, u32[]{:S(2)}, u32[]{:S(2)}) async-start(bf16[64,1,1]{2,1,0:T(2,128)(2,1)} %convert_element_type.80), calls=%async_computation.1 | async-start | bytes 65536 | tf_op jit(solution)/shard_map/all_to_all | solution.py:55
  34.9 13.1 %copy-start.1 = (f32[1,128,16]{1,2,0:T(8,128)S(1)}, f32[1,128,16]{1,2,0:T(8,128)}, u32[]{:S(2)}) copy-start(f32[1,128,16]{1,2,0:T(8,128)} %param.8) | copy-start | bytes 24580
  34.9 88.7 %all-to-all-start = ((bf16[64,24,1024]{2,1,0:T(8,128)(2,1)}), bf16[64,24,1024]{2,1,0:T(8,128)(2,1)}, u32[]{:S(2)}, u32[]{:S(2)}) async-start(bf16[64,24,1024]{2,1,0:T(8,128)(2,1)} %bitcast.47), calls=%async_computation | async-start | bytes 6291456 | tf_op jit(solution)/shard_map/all_to_all | solution.py:54
  128.0 37.0 %all-to-all-start.2 = ((f32[64,1,24]{2,1,0:T(1,128)}), f32[64,1,24]{2,1,0:T(1,128)S(1)}, u32[]{:S(2)}, u32[]{:S(2)}) async-start(f32[64,1,24]{2,1,0:T(1,128)} %bitcast.12), calls=%async_computation.2 | async-start | bytes 65536 | tf_op jit(solution)/shard_map/all_to_all | solution.py:62
where the time goes:
time: 166 us
  waiting for transfers between devices  79.9 us (48%)
  starting transfers between devices  55.6 us (33%)
  local copies, waits for them, and re-layouts  13.8 us (8%)
  other arithmetic  12.1 us (7%)
  matrix products  4.27 us (3%)
    all_to_all x1, waiting for transfers between devices, local(): lax.all_to_all(packed, 'expert', split_axis=0, concat_axis=0, tiled=True)  68 us
    all_to_all x1, starting transfers between devices, local(): lax.all_to_all(products, 'expert', split_axis=0, concat_axis=0, tiled=True)  25 us
    all_to_all x1, starting transfers between devices, local(): lax.all_to_all(count_column.astype(jnp.bfloat16), 'expert', split_axis=0,...  16.6 us
    all_to_all x1, starting transfers between devices, local(): lax.all_to_all(packed, 'expert', split_axis=0, concat_axis=0, tiled=True)  13.1 us
    all_to_all x1, waiting for transfers between devices, local(): lax.all_to_all(products, 'expert', split_axis=0, concat_axis=0, tiled=True)  11.9 us
    gather x1, local copies, waits for them, and re-layouts, owner_rows(): jnp.take(saved, jnp.minimum(position, saved.shape[0] - 1), axis=0)  5.9 us
    dot_general x1, other arithmetic, local(): jnp.einsum('jkq,jkq->jk', arrived, saved_rows, preferred_element_type=jnp...  4.35 us
  transfers between devices with their start and end apart: 5, of which 2 were waited for; matrix products, arithmetic and copies ran while one was open for 15% of the time, Pallas kernels for 0%

commit v1 on v0

v1 whole, which is shorter than its diff:
```python
import functools

import jax
import jax.numpy as jnp
from jax import lax
from jax.experimental import pallas as pl
from jax.experimental.pallas import tpu as pltpu
from jax.sharding import PartitionSpec as P

ROWS = 8
COLS = 8
NEAR = (1, -1, 2, -2, 3, -3, 0)
WIDE = 2
META = 16
VMEM = pl.BlockSpec(memory_space=pltpu.VMEM)
SMEM = pl.BlockSpec(memory_space=pltpu.SMEM)
ANY = pl.BlockSpec(memory_space=pl.ANY)


def along_section(x, by):
    n = lax.axis_size("section")
    return lax.ppermute(x, "section", [(i, (i + by) % n) for i in range(n)])


def along_y(x, by):
    return lax.ppermute(
        x, "expert", [(i, (i + COLS * by) % (ROWS * COLS)) for i in range(ROWS * COLS)]
    )


def along_z(x, step):
    return lax.ppermute(
        x,
        "expert",
        [(i, (i // COLS) * COLS + (i + step(i % COLS)) % COLS) for i in range(ROWS * COLS)],
    )


def exchange_z(x):
    groups = [[y * COLS + z for z in range(COLS)] for y in range(ROWS)]
    return lax.all_to_all(
        x, "expert", split_axis=0, concat_axis=0, axis_index_groups=groups, tiled=True
    )


def two_away(z):
    return 2 if z % 2 == 0 else -2


def wrap(i, n):
    return lax.rem(i + n, n)


def call(kernel, out_shape, specs, cost=1, **kw):
    return pl.pallas_call(
        kernel,
        out_shape=out_shape,
        in_specs=specs,
        out_specs=jax.tree.map(lambda _: VMEM, out_shape),
        compiler_params=pltpu.CompilerParams(vmem_limit_bytes=16 * 1024 * 1024),
        cost_estimate=pl.CostEstimate(flops=cost, bytes_accessed=1 << 20, transcendentals=0),
        **kw,
    )


def slab_kernel(cap, steps, counts_ref, place_ref, saved_ref, *refs):
    n = len(steps)
    outs, (offsets, windows, slabs, reads, writes) = refs[:n], refs[n:]
    total = saved_ref.shape[0]
    slab = cap * COLS
    reach = slab + 16
    y = place_ref[0] // COLS

    def add(i, before):
        offsets[i] = before
        return before + counts_ref[i]

    lax.fori_loop(0, ROWS * COLS, add, jnp.int32(0))
    rows = [wrap(y + by, ROWS) for by in steps]
    bases = [
        pl.multiple_of(jnp.minimum((offsets[r * COLS] // 16) * 16, total - reach), 16) for r in rows
    ]
    fetch = [
        pltpu.make_async_copy(saved_ref.at[pl.ds(bases[k], reach)], windows.at[k], reads.at[k])
        for k in range(n)
    ]
    store = [pltpu.make_async_copy(slabs.at[k], outs[k], writes.at[k]) for k in range(n)]
    for f in fetch:
        f.start()
    line = lax.broadcasted_iota(jnp.int32, (slab, reach), 0)
    lane = lax.broadcasted_iota(jnp.int32, (slab, reach), 1)
    for k, by in enumerate(steps):
        if by == 4:
            at = jnp.zeros((slab, reach), jnp.int32)
            for c in range(COLS):
                shift = offsets[rows[k] * COLS + c] - bases[k] - c * cap
                at = jnp.where((line >= c * cap) & (line < (c + 1) * cap), line + shift, at)
        else:
            at = line + (offsets[rows[k] * COLS] - bases[k])
        fetch[k].wait()
        slabs[k] = jnp.dot(
            (lane == at).astype(jnp.bfloat16), windows[k], preferred_element_type=jnp.float32
        ).astype(jnp.bfloat16)
        store[k].start()
    for w in store:
        w.wait()


def cut_slabs(cap, steps, counts, place, saved):
    slab, width = cap * COLS, saved.shape[1]
    n = len(steps)
    return pl.pallas_call(
        functools.partial(slab_kernel, cap, steps),
        out_shape=[jax.ShapeDtypeStruct((slab, width), saved.dtype)] * n,
        in_specs=[SMEM, SMEM, ANY],
        out_specs=[ANY] * n,
        scratch_shapes=[
            pltpu.SMEM((ROWS * COLS,), jnp.int32),
            pltpu.VMEM((n, slab + 16, width), saved.dtype),
            pltpu.VMEM((n, slab, width), saved.dtype),
            pltpu.SemaphoreType.DMA((n,)),
            pltpu.SemaphoreType.DMA((n,)),
        ],
        compiler_params=pltpu.CompilerParams(vmem_limit_bytes=16 * 1024 * 1024),
        cost_estimate=pl.CostEstimate(
            flops=n * 2 * slab * (slab + 16) * width,
            bytes_accessed=n * 4 * slab * width,
            transcendentals=0,
        ),
    )(counts, place, saved)


def payload_kernel(place_ref, codes_ref, meta_ref, own_ref, up_ref, down_ref, two_ref):
    z = wrap(place_ref[0], COLS)
    quarter = own_ref.shape[0] - META
    for by, out in ((0, own_ref), (1, up_ref), (3, down_ref), (2, two_ref)):
        q = lax.rem(z + by, 4)
        part = codes_ref[:, pl.ds(pl.multiple_of(q * quarter, quarter), quarter)]
        out[:quarter] = part.T
        out[quarter:] = meta_ref[...]


def gather_kernel(*refs):
    blocks, out_ref = refs[:-1], refs[-1]
    tokens = blocks[0].shape[1]
    for j, block in enumerate(blocks):
        out_ref[:, j * tokens : (j + 1) * tokens] = block[...]


def columns_of(z):
    odd = lax.rem(z, 2) == 1
    two = jnp.where(odd, z + 2, z - 2)
    return [
        lax.rem(c + 2 * COLS, COLS)
        for c in (z, z - 1, z + 1, two, z + 4, z + 3, z + 5, two + 4)
    ]


def meet_kernel(steps, place_ref, first_ref, second_ref, *refs):
    slabs, out_ref = refs[:-1], refs[-1]
    slab = slabs[0].shape[0]
    tokens = out_ref.shape[2]
    y = place_ref[0] // COLS
    z = lax.rem(place_ref[0], COLS)
    half = z // 4
    column = columns_of(z)
    quarter = first_ref.shape[0] - META
    k_of = lax.broadcasted_iota(jnp.int32, (8, 1), 0)
    expert = jnp.full((8, 1), -1, jnp.int32)
    for k, by in enumerate(steps):
        expert = jnp.where(k_of == k, 2 * wrap(y - by, ROWS) + half, expert)
    expert = expert.astype(jnp.float32)
    notes = [r[quarter:].astype(jnp.float32) for r in (first_ref, second_ref)]

    def note(i, j):
        return notes[j // 4][i : i + 1, (j % 4) * tokens : (j % 4 + 1) * tokens]

    hits = [[note(i, j) == expert for i in range(2)] for j in range(8)]
    loads = [
        jnp.sum((h[0] | h[1]).astype(jnp.float32), axis=1, keepdims=True) for h in hits
    ]
    wants = []
    for j in range(8):
        base = jnp.zeros((8, 1), jnp.float32)
        for i in range(8):
            if i != j:
                base = base + jnp.where(column[i] < column[j], loads[i], 0.0)
        wants.append(
            jnp.where(hits[j][0], note(2, j) + base, jnp.where(hits[j][1], note(3, j) + base, -1.0))
        )
    line = lax.broadcasted_iota(jnp.int32, (slab, tokens), 0).astype(jnp.float32)
    rows = [[] for _ in range(8)]
    for k, slab_ref in enumerate(slabs):
        for g, codes_ref in enumerate((first_ref, second_ref)):
            scores = jnp.dot(
                slab_ref[...], codes_ref[:quarter], preferred_element_type=jnp.float32
            )
            for j in range(4):
                mask = line == wants[g * 4 + j][k : k + 1]
                picked = jnp.where(mask, scores[:, j * tokens : (j + 1) * tokens], 0.0)
                rows[g * 4 + j].append(jnp.sum(picked, axis=0, keepdims=True))
    for j in range(8):
        out_ref[column[j]] = jnp.concatenate(rows[j], axis=0)


def finish_kernel(
    cap, place_ref, back_ref, direct_ref, codes_ref, meta_ref, scales_ref, logits_ref, out_ref, gate_ref
):
    tokens = codes_ref.shape[0]
    quarter = direct_ref.shape[1]
    y = place_ref[0] // COLS
    meta = meta_ref[...].astype(jnp.float32)
    named, slots = [meta[0:1], meta[1:2]], [meta[2:3], meta[3:4]]
    scores = [
        lax.dot_general(
            direct_ref[...], codes_ref[:, q * quarter : (q + 1) * quarter],
            (((1,), (1,)), ((), ())), preferred_element_type=jnp.float32,
        )
        for q in range(4)
    ]
    line = lax.broadcasted_iota(jnp.int32, (cap, tokens), 0).astype(jnp.float32)
    for half in range(2):
        sums = back_ref[half * 4]
        for q in range(1, 4):
            sums = sums + back_ref[half * 4 + q]
        for k, by in enumerate(NEAR):
            gate_ref[pl.ds(2 * wrap(y - by, ROWS) + half, 1)] = sums[k : k + 1]
        far = 2 * wrap(y + 4, ROWS) + half
        far_f = far.astype(jnp.float32)
        want = jnp.where(named[0] == far_f, slots[0], jnp.where(named[1] == far_f, slots[1], -1.0))
        total = jnp.zeros((cap, tokens), jnp.float32)
        for q in range(4):
            at = (half * 4 + q) * cap
            total = total + scores[q][at : at + cap]
        gate_ref[pl.ds(far, 1)] = jnp.sum(
            jnp.where(line == want, total, 0.0), axis=0, keepdims=True
        )
    gate = gate_ref[...] * scales_ref[...]
    logits = logits_ref[...]
    powers = jnp.exp(logits - jnp.max(logits, axis=0, keepdims=True))
    probs = powers / jnp.sum(powers, axis=0, keepdims=True)
    out_ref[...] = probs * (gate - jnp.sum(probs * gate, axis=0, keepdims=True))


def local(grad_codes, grad_scales, routes, router_logits, expert_outputs):
    codes, scales = along_section(grad_codes[0], -1), along_section(grad_scales[0], -1)
    saved = expert_outputs[0, 0]
    place = lax.axis_index("expert").astype(jnp.int32)[None]
    cap = saved.shape[0] // (ROWS * COLS)
    slab = cap * COLS
    quarter = saved.shape[1]
    tokens = codes.shape[0]
    experts = router_logits.shape[2]
    bf16, f32 = jnp.bfloat16, jnp.float32

    chosen = routes[0].T
    ids = jnp.arange(experts, dtype=jnp.int32)
    hits = [(chosen[c][None] == ids[:, None]).astype(f32) for c in range(2)]
    counts = jnp.sum(hits[0] + hits[1], axis=1)
    load = lax.all_to_all(
        jnp.broadcast_to(jnp.repeat(counts, 4)[:, None, None].astype(jnp.int32), (64, WIDE, 128)),
        "expert", split_axis=0, concat_axis=0, tiled=True,
    )[:, 0, 0]

    upper = (jnp.arange(tokens)[:, None] < jnp.arange(tokens)[None]).astype(f32)
    before = jnp.dot(hits[0] + hits[1], upper)
    slots = [jnp.sum(h * before, axis=0) for h in hits]
    meta = jnp.stack([chosen[0].astype(f32), chosen[1].astype(f32)] + slots)
    meta = jnp.pad(meta, ((0, META - 4), (0, 0))).astype(bf16)

    block = jax.ShapeDtypeStruct((quarter + META, tokens), bf16)
    own, up, down, two = call(payload_kernel, [block] * 4, [SMEM, VMEM, VMEM])(place, codes, meta)
    up = along_z(up, lambda z: 1)
    down = along_z(down, lambda z: -1)
    two = along_z(two, two_away)

    ready, own = lax.optimization_barrier((place, own))
    *mine, pieces = cut_slabs(cap, (1, -1, 4), load, ready, saved)
    ready, mine[0] = lax.optimization_barrier((ready, mine[0]))
    mine = mine + list(cut_slabs(cap, (2, -2, 3, -3, 0), load, ready, saved))
    arrived = [along_y(mine[k], NEAR[k]) for k in range(4)]
    for k in (4, 5):
        payload, arrived[k - 4] = lax.optimization_barrier((mine[k], arrived[k - 4]))
        arrived.append(along_y(payload, NEAR[k]))
    arrived.append(mine[6])
    far, arrived[2] = lax.optimization_barrier(
        (exchange_z(pieces.reshape(COLS, cap, quarter)).reshape(slab, quarter), arrived[2])
    )
    direct = along_y(far, 4)

    own, arrived[6] = lax.optimization_barrier((own, arrived[6]))
    first = call(
        gather_kernel, jax.ShapeDtypeStruct((quarter + META, 4 * tokens), bf16), [VMEM] * 4
    )(own, up, down, two)
    second = along_z(first, lambda z: 4)

    def meet(steps, slabs):
        return call(
            functools.partial(meet_kernel, steps),
            jax.ShapeDtypeStruct((COLS, len(steps), tokens), f32), [SMEM] + [VMEM] * (2 + len(steps)),
            cost=2 * len(steps) * slab * quarter * COLS * tokens,
        )(place, first, second, *slabs)

    parts = jnp.concatenate([meet(NEAR, arrived), jnp.zeros((COLS, 1, tokens), f32)], axis=1)
    returned = exchange_z(parts)
    logit_grad = call(
        functools.partial(finish_kernel, cap),
        jax.ShapeDtypeStruct((experts, tokens), f32), [SMEM] + [VMEM] * 6,
        scratch_shapes=[pltpu.VMEM((experts, tokens), f32)],
    )(place, returned, direct, codes, meta, scales.astype(f32)[None], router_logits[0].T)
    return logit_grad.T[None]


def solution(mesh):
    placed = (
        P("section", "expert", None),
        P("section", "expert"),
        P("section", "expert", None),
        P("section", "expert", None),
        P("section", "expert", None, None),
    )
    return jax.shard_map(
        local, mesh=mesh, in_specs=placed, out_specs=P("section", "expert", None), check_vma=False
    )
```

time: 166 us -> 156 us (0.940)
  the two profiles are of different devices: /device:TPU:6 before, /device:TPU:14 now
where the time goes in v1:
time: 156 us; the launch traced here: 155 us
  starting transfers between devices  90.1 us (58%)
  waiting for transfers between devices  40.2 us (26%)
  Pallas kernels  14.2 us (9%)
  local copies, waits for them, and re-layouts  9.16 us (6%)
    all_to_all x2, waiting for transfers between devices, exchange_z(): lax.all_to_all(x, 'expert', split_axis=0, concat_axis=0, axis_index_group...  35.8 us
    all_to_all x2, starting transfers between devices, exchange_z(): lax.all_to_all(x, 'expert', split_axis=0, concat_axis=0, axis_index_group...  29.2 us
    ppermute x7, starting transfers between devices, along_y(): lax.ppermute(x, 'expert', [(i, (i + COLS * by) % (ROWS * COLS)) for i in...  28.4 us
    all_to_all x1, starting transfers between devices, local(): lax.all_to_all(jnp.broadcast_to(jnp.repeat(counts, 4)[:, None, None].asty...  16.6 us
    ppermute x4, starting transfers between devices, along_z(): lax.ppermute(x, 'expert', [(i, i // COLS * COLS + (i + step(i % COLS)) %...  15.6 us
    pallas_call x2, Pallas kernels, cut_slabs(): pl.pallas_call(functools.partial(slab_kernel, cap, steps), out_shape=[jax...  7.81 us
    unnamed x22, local copies, waits for them, and re-layouts  6.36 us
    pallas_call x1, Pallas kernels, meet(): call(functools.partial(meet_kernel, steps), jax.ShapeDtypeStruct((COLS, l...  4.67 us
  transfers between devices with their start and end apart: 16, of which 4 were waited for; matrix products, arithmetic and copies ran while one was open for 2% of the time, Pallas kernels for 8%

profile of v1, /device:TPU:14, one launch (start us, length us, event | category | flops | bytes accessed | tf_op | source)
XLA Modules:
  0.0 154.9 jit_solution(5733499290800457134)
XLA Ops:
  2.1 16.6 %all-to-all-start = ((s32[64,2,128]{2,1,0:T(2,128)}), s32[64,2,128]{2,1,0:T(2,128)S(1)}, u32[]{:S(2)}, u32[]{:S(2)}) async-start(s32[64,2,128]{2,1,0:T(2,128)} %broadcast_in_dim.26), calls=%async_computation | async-start | bytes 131072 | tf_op jit(solution)/shard_map/all_to_all | solution.py:260
  19.1 3.4 %collective-permute-start.1 = (bf16[1040,128]{1,0:T(8,128)(2,1)S(1)}, bf16[1040,128]{1,0:T(8,128)(2,1)S(1)}, u32[]{:S(2)}, u32[]{:S(2)}) collective-permute-start(bf16[1040,128]{1,0:T(8,128)(2,1)S(1)} %get-tuple-element.36), channel_id=1, source_target_pairs={{0,1},{1,2},{2,3},{3,4},{4,5},{5,6},{6,7},{7,0},{8,9},{9,10},{10,1... | collective-permute-start | bytes 798728 | tf_op jit(solution)/shard_map/ppermute | solution.py:32
  22.5 3.7 %collective-permute-start.2 = (bf16[1040,128]{1,0:T(8,128)(2,1)S(1)}, bf16[1040,128]{1,0:T(8,128)(2,1)S(1)}, u32[]{:S(2)}, u32[]{:S(2)}) collective-permute-start(bf16[1040,128]{1,0:T(8,128)(2,1)S(1)} %get-tuple-element.37), channel_id=1, source_target_pairs={{0,7},{1,0},{2,1},{3,2},{4,3},{5,4},{6,5},{7,6},{8,15},{9,8},{10,9... | collective-permute-start | bytes 798728 | tf_op jit(solution)/shard_map/ppermute | solution.py:32
  26.1 3.1 %collective-permute-start.3 = (bf16[1040,128]{1,0:T(8,128)(2,1)S(1)}, bf16[1040,128]{1,0:T(8,128)(2,1)S(1)}, u32[]{:S(2)}, u32[]{:S(2)}) collective-permute-start(bf16[1040,128]{1,0:T(8,128)(2,1)S(1)} %get-tuple-element.38), channel_id=1, source_target_pairs={{0,2},{1,7},{2,4},{3,1},{4,6},{5,3},{6,0},{7,5},{8,10},{9,15},{10,... | collective-permute-start | bytes 798728 | tf_op jit(solution)/shard_map/ppermute | solution.py:32
  29.9 1.3 slice_reduce_fusion.counts_ref
  31.1 1.9 %copy-done = bf16[1,1,1536,1024]{3,2,1,0:T(8,128)(2,1)S(1)} copy-done((bf16[1,1,1536,1024]{3,2,1,0:T(8,128)(2,1)S(1)}, bf16[1,1,1536,1024]{3,2,1,0:T(8,128)(2,1)}, u32[]{:S(2)}) %copy-start) | copy-done | bytes 3145752
  33.0 3.3 %shard_map.56 = (bf16[192,1024]{1,0:T(8,128)(2,1)}, bf16[192,1024]{1,0:T(8,128)(2,1)}, bf16[192,1024]{1,0:T(8,128)(2,1)}) custom-call(s32[64]{0:T(128)S(1)} %slice_reduce_fusion.counts_ref, s32[1]{0:T(128)} %bitcast.place_ref, bf16[1536,1024]{1,0:T(8,128)(2,1)S(1)} %bitcast.28), custom_call_target="tpu_custom_call" | custom-call | flops 245366784 | bytes 2359296 | tf_op jit(solution)/shard_map/pallas_call | solution.py:112
  36.3 4.5 %shard_map.57 = (bf16[192,1024]{1,0:T(8,128)(2,1)S(1)}, bf16[192,1024]{1,0:T(8,128)(2,1)S(1)}, bf16[192,1024]{1,0:T(8,128)(2,1)S(1)}, bf16[192,1024]{1,0:T(8,128)(2,1)S(1)}, bf16[192,1024]{1,0:T(8,128)(2,1)S(1)}) custom-call(s32[64]{0:T(128)S(1)} %slice_reduce_fusion.counts_ref, s32[1]{0:T(128)} %bitcast.place_ref, bf16[1536,1024]{1,0:T(8,128)(2,1)S(1)} %bitcast.29), custom_call_target="tpu_custom_call" | custom-call | flops 408944640 | bytes 3932160 | tf_op jit(solution)/shard_map/pallas_call | solution.py:112
  42.8 5.5 %collective-permute-start.4 = (bf16[1040,512]{1,0:T(8,128)(2,1)S(1)}, bf16[1040,512]{1,0:T(8,128)(2,1)}, u32[]{:S(2)}, u32[]{:S(2)}) collective-permute-start(bf16[1040,512]{1,0:T(8,128)(2,1)S(1)} %shard_map.58.first_ref), channel_id=1, source_target_pairs={{0,4},{1,5},{2,6},{3,7},{4,0},{5,1},{6,2},{7,3},{8,12},{9,13},{10,... | collective-permute-start | bytes 3194888 | tf_op jit(solution)/shard_map/ppermute | solution.py:32
  48.3 3.4 %collective-permute-start.5 = (bf16[192,1024]{1,0:T(8,128)(2,1)}, bf16[192,1024]{1,0:T(8,128)(2,1)S(1)}, u32[]{:S(2)}, u32[]{:S(2)}) collective-permute-start(bf16[192,1024]{1,0:T(8,128)(2,1)} %get-tuple-element.40), channel_id=1, source_target_pairs={{0,8},{1,9},{2,10},{3,11},{4,12},{5,13},{6,14},{7,15},{8,16},{9,17... | collective-permute-start | bytes 1179656 | tf_op jit(solution)/shard_map/ppermute | solution.py:26
  51.7 2.4 %collective-permute-start.6 = (bf16[192,1024]{1,0:T(8,128)(2,1)}, bf16[192,1024]{1,0:T(8,128)(2,1)S(1)}, u32[]{:S(2)}, u32[]{:S(2)}) collective-permute-start(bf16[192,1024]{1,0:T(8,128)(2,1)} %get-tuple-element.43), channel_id=1, source_target_pairs={{0,56},{1,57},{2,58},{3,59},{4,60},{5,61},{6,62},{7,63},{8,0},{9,1... | collective-permute-start | bytes 1179656 | tf_op jit(solution)/shard_map/ppermute | solution.py:26
  54.2 5.4 %all-to-all-start.1 = ((bf16[8,24,1024]{2,1,0:T(8,128)(2,1)}), bf16[8,24,1024]{2,1,0:T(8,128)(2,1)}, u32[]{:S(2)}, u32[]{:S(2)}) async-start(bf16[8,24,1024]{2,1,0:T(8,128)(2,1)} %bitcast.10), calls=%async_computation.1 | async-start | bytes 786432 | tf_op jit(solution)/shard_map/all_to_all | solution.py:41
  59.6 5.0 %collective-permute-start.7 = (bf16[192,1024]{1,0:T(8,128)(2,1)}, bf16[192,1024]{1,0:T(8,128)(2,1)S(1)}, u32[]{:S(2)}, u32[]{:S(2)}) collective-permute-start(bf16[192,1024]{1,0:T(8,128)(2,1)} %copy-done.7), channel_id=1, source_target_pairs={{0,16},{1,17},{2,18},{3,19},{4,20},{5,21},{6,22},{7,23},{8,24},{9,... | collective-permute-start | bytes 1179656 | tf_op jit(solution)/shard_map/ppermute | solution.py:26
  64.7 2.9 %collective-permute-start.8 = (bf16[192,1024]{1,0:T(8,128)(2,1)}, bf16[192,1024]{1,0:T(8,128)(2,1)}, u32[]{:S(2)}, u32[]{:S(2)}) collective-permute-start(bf16[192,1024]{1,0:T(8,128)(2,1)} %copy-done.6), channel_id=1, source_target_pairs={{0,48},{1,49},{2,50},{3,51},{4,52},{5,53},{6,54},{7,55},{8,56},{9,... | collective-permute-start | bytes 1179656 | tf_op jit(solution)/shard_map/ppermute | solution.py:26
  67.6 5.0 %collective-permute-start.10 = (bf16[192,1024]{1,0:T(8,128)(2,1)}, bf16[192,1024]{1,0:T(8,128)(2,1)}, u32[]{:S(2)}, u32[]{:S(2)}) collective-permute-start(bf16[192,1024]{1,0:T(8,128)(2,1)} %copy-done.5), channel_id=1, source_target_pairs={{0,40},{1,41},{2,42},{3,43},{4,44},{5,45},{6,46},{7,47},{8,48},{9,... | collective-permute-start | bytes 1179656 | tf_op jit(solution)/shard_map/ppermute | solution.py:26
  72.6 4.6 %collective-permute-start.9 = (bf16[192,1024]{1,0:T(8,128)(2,1)}, bf16[192,1024]{1,0:T(8,128)(2,1)}, u32[]{:S(2)}, u32[]{:S(2)}) collective-permute-start(bf16[192,1024]{1,0:T(8,128)(2,1)} %copy-done.4), channel_id=1, source_target_pairs={{0,24},{1,25},{2,26},{3,27},{4,28},{5,29},{6,30},{7,31},{8,32},{9,... | collective-permute-start | bytes 1179656 | tf_op jit(solution)/shard_map/ppermute | solution.py:26
  78.0 27.8 %all-to-all-done.1 = bf16[8,24,1024]{2,1,0:T(8,128)(2,1)} async-done(((bf16[8,24,1024]{2,1,0:T(8,128)(2,1)}), bf16[8,24,1024]{2,1,0:T(8,128)(2,1)}, u32[]{:S(2)}, u32[]{:S(2)}) %all-to-all-start.1) | async-done | bytes 393248 | tf_op jit(solution)/shard_map/all_to_all | solution.py:41
  105.8 5.0 %collective-permute-start.11 = (bf16[192,1024]{1,0:T(8,128)(2,1)}, bf16[192,1024]{1,0:T(8,128)(2,1)S(1)}, u32[]{:S(2)}, u32[]{:S(2)}) collective-permute-start(bf16[192,1024]{1,0:T(8,128)(2,1)} %bitcast.11), channel_id=1, source_target_pairs={{0,32},{1,33},{2,34},{3,35},{4,36},{5,37},{6,38},{7,39},{8,40},{9,... | collective-permute-start | bytes 1179656 | tf_op jit(solution)/shard_map/ppermute | solution.py:26
  110.9 3.7 %collective-permute-done.10.refs_5_ = bf16[192,1024]{1,0:T(8,128)(2,1)} collective-permute-done((bf16[192,1024]{1,0:T(8,128)(2,1)}, bf16[192,1024]{1,0:T(8,128)(2,1)}, u32[]{:S(2)}, u32[]{:S(2)}) %collective-permute-start.10) | collective-permute-done | bytes 393248 | tf_op jit(solution)/shard_map/ppermute | solution.py:26
  114.6 1.0 copy-done.3
  116.6 4.7 %shard_map.59 = f32[8,7,128]{2,1,0:T(8,128)S(1)} custom-call(s32[1]{0:T(128)} %bitcast.place_ref, bf16[1040,512]{1,0:T(8,128)(2,1)S(1)} %shard_map.58.first_ref, bf16[1040,512]{1,0:T(8,128)(2,1)} %collective-permute-done.4.second_ref, bf16[192,1024]{1,0:T(8,128)(2,1)S(1)} %collective-permute-done.5.refs_0_, ...), custom_call_target="tpu_custom_call" | custom-call | flops 2818572288 | bytes 1048576 | tf_op jit(solution)/shard_map/pallas_call | solution.py:298
  121.9 23.8 %all-to-all-start.2 = ((f32[8,8,128]{2,1,0:T(8,128)}), f32[8,8,128]{2,1,0:T(8,128)S(1)}, u32[]{:S(2)}, u32[]{:S(2)}) async-start(f32[8,8,128]{2,1,0:T(8,128)} %concatenate.3), calls=%async_computation.2 | async-start | bytes 65536 | tf_op jit(solution)/shard_map/all_to_all | solution.py:41
  145.7 8.0 %all-to-all-done.2.back_ref = f32[8,8,128]{2,1,0:T(8,128)S(1)} async-done(((f32[8,8,128]{2,1,0:T(8,128)}), f32[8,8,128]{2,1,0:T(8,128)S(1)}, u32[]{:S(2)}, u32[]{:S(2)}) %all-to-all-start.2) | async-done | bytes 32800 | tf_op jit(solution)/shard_map/all_to_all | solution.py:41
  153.7 1.2 shard_map.60
  (46 shorter events, 7.4 us)
Async XLA Ops:
  0.0 18.7 %collective-permute-start = (bf16[128,4096]{1,0:T(8,128)(2,1)}, bf16[128,4096]{1,0:T(8,128)(2,1)S(1)}, u32[]{:S(2)}, u32[]{:S(2)}) collective-permute-start(bf16[128,4096]{1,0:T(8,128)(2,1)} %bitcast.34), channel_id=1, source_target_pairs={{0,448},{64,0},{128,64},{192,128},{256,192},{320,256},{384,320},{4... | collective-permute-start | bytes 3145736 | tf_op jit(solution)/shard_map/ppermute | solution.py:22
  2.1 27.8 %all-to-all-start = ((s32[64,2,128]{2,1,0:T(2,128)}), s32[64,2,128]{2,1,0:T(2,128)S(1)}, u32[]{:S(2)}, u32[]{:S(2)}) async-start(s32[64,2,128]{2,1,0:T(2,128)} %broadcast_in_dim.26), calls=%async_computation | async-start | bytes 131072 | tf_op jit(solution)/shard_map/all_to_all | solution.py:260
  19.1 22.6 %collective-permute-start.1 = (bf16[1040,128]{1,0:T(8,128)(2,1)S(1)}, bf16[1040,128]{1,0:T(8,128)(2,1)S(1)}, u32[]{:S(2)}, u32[]{:S(2)}) collective-permute-start(bf16[1040,128]{1,0:T(8,128)(2,1)S(1)} %get-tuple-element.36), channel_id=1, source_target_pairs={{0,1},{1,2},{2,3},{3,4},{4,5},{5,6},{6,7},{7,0},{8,9},{9,10},{10,1... | collective-permute-start | bytes 798728 | tf_op jit(solution)/shard_map/ppermute | solution.py:32
  22.5 19.2 %collective-permute-start.2 = (bf16[1040,128]{1,0:T(8,128)(2,1)S(1)}, bf16[1040,128]{1,0:T(8,128)(2,1)S(1)}, u32[]{:S(2)}, u32[]{:S(2)}) collective-permute-start(bf16[1040,128]{1,0:T(8,128)(2,1)S(1)} %get-tuple-element.37), channel_id=1, source_target_pairs={{0,7},{1,0},{2,1},{3,2},{4,3},{5,4},{6,5},{7,6},{8,15},{9,8},{10,9... | collective-permute-start | bytes 798728 | tf_op jit(solution)/shard_map/ppermute | solution.py:32
  26.1 15.5 %collective-permute-start.3 = (bf16[1040,128]{1,0:T(8,128)(2,1)S(1)}, bf16[1040,128]{1,0:T(8,128)(2,1)S(1)}, u32[]{:S(2)}, u32[]{:S(2)}) collective-permute-start(bf16[1040,128]{1,0:T(8,128)(2,1)S(1)} %get-tuple-element.38), channel_id=1, source_target_pairs={{0,2},{1,7},{2,4},{3,1},{4,6},{5,3},{6,0},{7,5},{8,10},{9,15},{10,... | collective-permute-start | bytes 798728 | tf_op jit(solution)/shard_map/ppermute | solution.py:32
  31.1 1.9 %copy-start = (bf16[1,1,1536,1024]{3,2,1,0:T(8,128)(2,1)S(1)}, bf16[1,1,1536,1024]{3,2,1,0:T(8,128)(2,1)}, u32[]{:S(2)}) copy-start(bf16[1,1,1536,1024]{3,2,1,0:T(8,128)(2,1)} %param.9) | copy-start | bytes 9437188
  41.6 0.9 copy-start.5
  41.6 1.1 copy-start.6
  41.6 1.2 copy-start.7
  41.6 36.4 %copy-start.10 = (bf16[1,128]{1,0:T(2,128)(2,1)S(1)}, bf16[1,128]{1,0:T(2,128)(2,1)}, u32[]{:S(2)}) copy-start(bf16[1,128]{1,0:T(2,128)(2,1)} %param.6) | copy-start | bytes 772
  42.8 71.7 %collective-permute-start.4 = (bf16[1040,512]{1,0:T(8,128)(2,1)S(1)}, bf16[1040,512]{1,0:T(8,128)(2,1)}, u32[]{:S(2)}, u32[]{:S(2)}) collective-permute-start(bf16[1040,512]{1,0:T(8,128)(2,1)S(1)} %shard_map.58.first_ref), channel_id=1, source_target_pairs={{0,4},{1,5},{2,6},{3,7},{4,0},{5,1},{6,2},{7,3},{8,12},{9,13},{10,... | collective-permute-start | bytes 3194888 | tf_op jit(solution)/shard_map/ppermute | solution.py:32
  48.3 19.3 %collective-permute-start.5 = (bf16[192,1024]{1,0:T(8,128)(2,1)}, bf16[192,1024]{1,0:T(8,128)(2,1)S(1)}, u32[]{:S(2)}, u32[]{:S(2)}) collective-permute-start(bf16[192,1024]{1,0:T(8,128)(2,1)} %get-tuple-element.40), channel_id=1, source_target_pairs={{0,8},{1,9},{2,10},{3,11},{4,12},{5,13},{6,14},{7,15},{8,16},{9,17... | collective-permute-start | bytes 1179656 | tf_op jit(solution)/shard_map/ppermute | solution.py:26
  51.7 15.9 %collective-permute-start.6 = (bf16[192,1024]{1,0:T(8,128)(2,1)}, bf16[192,1024]{1,0:T(8,128)(2,1)S(1)}, u32[]{:S(2)}, u32[]{:S(2)}) collective-permute-start(bf16[192,1024]{1,0:T(8,128)(2,1)} %get-tuple-element.43), channel_id=1, source_target_pairs={{0,56},{1,57},{2,58},{3,59},{4,60},{5,61},{6,62},{7,63},{8,0},{9,1... | collective-permute-start | bytes 1179656 | tf_op jit(solution)/shard_map/ppermute | solution.py:26
  54.2 51.6 %all-to-all-start.1 = ((bf16[8,24,1024]{2,1,0:T(8,128)(2,1)}), bf16[8,24,1024]{2,1,0:T(8,128)(2,1)}, u32[]{:S(2)}, u32[]{:S(2)}) async-start(bf16[8,24,1024]{2,1,0:T(8,128)(2,1)} %bitcast.10), calls=%async_computation.1 | async-start | bytes 786432 | tf_op jit(solution)/shard_map/all_to_all | solution.py:41
  59.6 17.6 %collective-permute-start.7 = (bf16[192,1024]{1,0:T(8,128)(2,1)}, bf16[192,1024]{1,0:T(8,128)(2,1)S(1)}, u32[]{:S(2)}, u32[]{:S(2)}) collective-permute-start(bf16[192,1024]{1,0:T(8,128)(2,1)} %copy-done.7), channel_id=1, source_target_pairs={{0,16},{1,17},{2,18},{3,19},{4,20},{5,21},{6,22},{7,23},{8,24},{9,... | collective-permute-start | bytes 1179656 | tf_op jit(solution)/shard_map/ppermute | solution.py:26
  64.7 41.2 %collective-permute-start.8 = (bf16[192,1024]{1,0:T(8,128)(2,1)}, bf16[192,1024]{1,0:T(8,128)(2,1)}, u32[]{:S(2)}, u32[]{:S(2)}) collective-permute-start(bf16[192,1024]{1,0:T(8,128)(2,1)} %copy-done.6), channel_id=1, source_target_pairs={{0,48},{1,49},{2,50},{3,51},{4,52},{5,53},{6,54},{7,55},{8,56},{9,... | collective-permute-start | bytes 1179656 | tf_op jit(solution)/shard_map/ppermute | solution.py:26
  67.6 47.0 %collective-permute-start.10 = (bf16[192,1024]{1,0:T(8,128)(2,1)}, bf16[192,1024]{1,0:T(8,128)(2,1)}, u32[]{:S(2)}, u32[]{:S(2)}) collective-permute-start(bf16[192,1024]{1,0:T(8,128)(2,1)} %copy-done.5), channel_id=1, source_target_pairs={{0,40},{1,41},{2,42},{3,43},{4,44},{5,45},{6,46},{7,47},{8,48},{9,... | collective-permute-start | bytes 1179656 | tf_op jit(solution)/shard_map/ppermute | solution.py:26
  72.6 41.9 %collective-permute-start.9 = (bf16[192,1024]{1,0:T(8,128)(2,1)}, bf16[192,1024]{1,0:T(8,128)(2,1)}, u32[]{:S(2)}, u32[]{:S(2)}) collective-permute-start(bf16[192,1024]{1,0:T(8,128)(2,1)} %copy-done.4), channel_id=1, source_target_pairs={{0,24},{1,25},{2,26},{3,27},{4,28},{5,29},{6,30},{7,31},{8,32},{9,... | collective-permute-start | bytes 1179656 | tf_op jit(solution)/shard_map/ppermute | solution.py:26
  78.0 67.7 %collective-permute-start.12 = (bf16[128]{0:T(256)(128)(2,1)S(1)}, bf16[128]{0:T(256)(128)(2,1)S(1)}, u32[]{:S(2)}, u32[]{:S(2)}) collective-permute-start(bf16[128]{0:T(256)(128)(2,1)S(1)} %bitcast.35), channel_id=1, source_target_pairs={{0,448},{64,0},{128,64},{192,128},{256,192},{320,256},{384,320},{4... | collective-permute-start | bytes 776 | tf_op jit(solution)/shard_map/ppermute | solution.py:22
  105.8 47.8 %copy-start.1 = (f32[1,128,16]{1,2,0:T(8,128)S(1)}, f32[1,128,16]{1,2,0:T(8,128)}, u32[]{:S(2)}) copy-start(f32[1,128,16]{1,2,0:T(8,128)} %param.8) | copy-start | bytes 24580
  105.8 39.8 %collective-permute-start.11 = (bf16[192,1024]{1,0:T(8,128)(2,1)}, bf16[192,1024]{1,0:T(8,128)(2,1)S(1)}, u32[]{:S(2)}, u32[]{:S(2)}) collective-permute-start(bf16[192,1024]{1,0:T(8,128)(2,1)} %bitcast.11), channel_id=1, source_target_pairs={{0,32},{1,33},{2,34},{3,35},{4,36},{5,37},{6,38},{7,39},{8,40},{9,... | collective-permute-start | bytes 1179656 | tf_op jit(solution)/shard_map/ppermute | solution.py:26
  114.6 1.0 copy-start.3
  115.6 1.0 copy-start.9
  121.9 31.8 %all-to-all-start.2 = ((f32[8,8,128]{2,1,0:T(8,128)}), f32[8,8,128]{2,1,0:T(8,128)S(1)}, u32[]{:S(2)}, u32[]{:S(2)}) async-start(f32[8,8,128]{2,1,0:T(8,128)} %concatenate.3), calls=%async_computation.2 | async-start | bytes 65536 | tf_op jit(solution)/shard_map/all_to_all | solution.py:41
  (3 other events, 2.3 us)

commit v2 on v0

v2 whole, which is shorter than its diff:
```python
import functools

import jax
import jax.numpy as jnp
from jax import lax
from jax.experimental import pallas as pl
from jax.experimental.pallas import tpu as pltpu
from jax.sharding import PartitionSpec as P

ROWS = 8
COLS = 8
PARTS = 4
WIDE = 2
LANES = 128
VMEM = pl.BlockSpec(memory_space=pltpu.VMEM)
SMEM = pl.BlockSpec(memory_space=pltpu.SMEM)
HBM = pl.BlockSpec(memory_space=pltpu.HBM)


def along_section(x, by):
    n = lax.axis_size("section")
    return lax.ppermute(x, "section", [(i, (i + by) % n) for i in range(n)])


def exchange(x):
    devices = ROWS * COLS
    order = [i * PARTS + q for q in range(PARTS) for i in range(devices // PARTS)]
    return lax.all_to_all(
        x, "expert", split_axis=0, concat_axis=0, axis_index_groups=[order], tiled=True
    )


def call(kernel, out_shape, in_specs, out_specs=None, flops=0, mib=1, **kw):
    return pl.pallas_call(
        kernel,
        out_shape=out_shape,
        in_specs=in_specs,
        out_specs=jax.tree.map(lambda _: VMEM, out_shape) if out_specs is None else out_specs,
        compiler_params=pltpu.CompilerParams(vmem_limit_bytes=60 * 1024 * 1024),
        cost_estimate=pl.CostEstimate(flops=flops, bytes_accessed=mib << 20, transcendentals=0),
        **kw,
    )


def count_kernel(routes_ref, out_ref):
    experts = out_ref.shape[0] // PARTS
    ids = lax.broadcasted_iota(jnp.int32, (experts, LANES), 0)
    hit = (routes_ref[0:1] == ids) | (routes_ref[1:2] == ids)
    counts = jnp.sum(hit.astype(jnp.int32), axis=1, keepdims=True)
    for o in range(out_ref.shape[0]):
        out_ref[o] = jnp.broadcast_to(counts[o // PARTS : o // PARTS + 1], (WIDE, LANES))


def slab_kernel(cap, counts_ref, saved_ref, out_ref, windows, wide, slabs, reads, writes):
    devices = ROWS * COLS
    total, reach, tail = saved_ref.shape[0], windows.shape[1], wide.shape[2]
    counts = counts_ref[:, 0].astype(jnp.float32)
    earlier = lax.broadcasted_iota(jnp.int32, (devices, devices), 1) < lax.broadcasted_iota(
        jnp.int32, (devices, devices), 0
    )
    offsets = jnp.dot(
        earlier.astype(jnp.float32), counts, preferred_element_type=jnp.float32,
        precision=lax.Precision.HIGHEST,
    ).astype(jnp.int32)
    at = [jnp.max(offsets[d : d + 1]) for d in range(devices)]
    bases, fetch = [], []
    for r in range(ROWS):
        base = jnp.minimum((at[r * COLS] // 16) * 16, total - reach)
        bases.append(pl.multiple_of(base, 16))
        fetch.append(
            pltpu.make_async_copy(
                saved_ref.at[pl.ds(bases[r], reach)], windows.at[r], reads.at[r]
            )
        )
        fetch[r].start()
    for b in range(2):
        wide[b, :, reach:] = jnp.zeros((wide.shape[1], tail - reach, LANES), jnp.float32)
    two = 2 * cap
    store = [
        pltpu.make_async_copy(
            slabs.at[:, pl.ds(r * two, two)], out_ref.at[:, pl.ds(r * two, two)], writes.at[r]
        )
        for r in range(ROWS)
    ]
    for r in range(ROWS):
        b = r % 2
        fetch[r].wait()
        for k in range(wide.shape[1]):
            wide[b, k, :reach] = windows[r, :, k * LANES : (k + 1) * LANES].astype(jnp.float32)
        for k in range(wide.shape[1]):
            for q in range(PARTS):
                rows = [
                    wide[b, k, pl.ds(at[r * COLS + c] - bases[r], cap), :]
                    for c in (q, q + PARTS)
                ]
                slabs[q, r * two : (r + 1) * two, k * LANES : (k + 1) * LANES] = jnp.concatenate(
                    rows, axis=0
                ).astype(jnp.bfloat16)
        store[r].start()
    for w in store:
        w.wait()


def finish_kernel(cap, routes_ref, scales_ref, logits_ref, codes_ref, rows_ref, out_ref, rows, sems):
    experts, tokens = logits_ref.shape
    quarter = rows.shape[2]
    fetch = [pltpu.make_async_copy(rows_ref.at[q], rows.at[q], sems.at[q]) for q in range(PARTS)]
    for f in fetch:
        f.start()
    ids = lax.broadcasted_iota(jnp.int32, (experts, tokens), 0)
    hit = (routes_ref[0:1] == ids) | (routes_ref[1:2] == ids)
    upper = lax.broadcasted_iota(jnp.int32, (tokens, tokens), 0) < lax.broadcasted_iota(
        jnp.int32, (tokens, tokens), 1
    )
    before = jnp.dot(
        hit.astype(jnp.float32), upper.astype(jnp.float32), preferred_element_type=jnp.float32
    )
    want = jnp.where(hit, before, -1.0)
    logits = logits_ref[...]
    powers = jnp.exp(logits - jnp.max(logits, axis=0, keepdims=True))
    probs = powers / jnp.sum(powers, axis=0, keepdims=True)
    scores = jnp.zeros((experts * cap, tokens), jnp.float32)
    for q in range(PARTS):
        fetch[q].wait()
        scores = scores + lax.dot_general(
            rows[q], codes_ref[:, q * quarter : (q + 1) * quarter], (((1,), (1,)), ((), ())),
            preferred_element_type=jnp.float32,
        )
    line = lax.broadcasted_iota(jnp.int32, (cap, tokens), 0).astype(jnp.float32)
    gate = jnp.concatenate(
        [
            jnp.sum(
                jnp.where(line == want[e : e + 1], scores[e * cap : (e + 1) * cap], 0.0),
                axis=0, keepdims=True,
            )
            for e in range(experts)
        ],
        axis=0,
    )
    gate = gate * scales_ref[...]
    out_ref[...] = probs * (gate - jnp.sum(probs * gate, axis=0, keepdims=True))


def local(grad_codes, grad_scales, routes, router_logits, expert_outputs):
    codes, scales = along_section(grad_codes[0], -1), along_section(grad_scales[0], -1)
    saved = expert_outputs[0, 0]
    devices = ROWS * COLS
    cap = saved.shape[0] // devices
    slab = cap * COLS
    quarter = saved.shape[1]
    tokens = codes.shape[0]
    experts = router_logits.shape[2]
    bf16, f32 = jnp.bfloat16, jnp.float32
    shape, dma = jax.ShapeDtypeStruct, pltpu.SemaphoreType.DMA

    chosen = routes[0].T
    load = lax.all_to_all(
        call(count_kernel, shape((devices, WIDE, LANES), jnp.int32), [VMEM])(chosen),
        "expert", split_axis=0, concat_axis=0, tiled=True,
    )
    mine = call(
        functools.partial(slab_kernel, cap), shape((PARTS, experts * cap, quarter), bf16),
        [VMEM, HBM], HBM, mib=6,
        scratch_shapes=[
            pltpu.VMEM((ROWS, slab + 16, quarter), bf16),
            pltpu.VMEM((2, quarter // LANES, slab + 16 + cap, LANES), f32),
            pltpu.VMEM((PARTS, experts * cap, quarter), bf16),
            dma((ROWS,)), dma((ROWS,)),
        ],
    )(load, saved)
    rows = exchange(mine.reshape(devices, cap, quarter)).reshape(PARTS, experts * cap, quarter)
    logit_grad = call(
        functools.partial(finish_kernel, cap), shape((experts, tokens), f32), [VMEM] * 4 + [HBM],
        scratch_shapes=[pltpu.VMEM((PARTS, experts * cap, quarter), bf16), dma((PARTS,))],
    )(chosen, scales.astype(f32)[None], router_logits[0].T, codes, rows)
    return logit_grad.T[None]


def solution(mesh):
    placed = (
        P("section", "expert", None),
        P("section", "expert"),
        P("section", "expert", None),
        P("section", "expert", None),
        P("section", "expert", None, None),
    )
    return jax.shard_map(
        local, mesh=mesh, in_specs=placed, out_specs=P("section", "expert", None), check_vma=False
    )
```

time: 166 us -> 125 us (0.75)
  the two profiles are of different devices: /device:TPU:6 before, /device:TPU:162 now
where the time goes in v2:
time: 125 us
  waiting for transfers between devices  79.7 us (64%)
  blocking collectives  20.2 us (16%)
  starting transfers between devices  12.1 us (10%)
  Pallas kernels  10.8 us (9%)
  local copies, waits for them, and re-layouts  1.66 us (1%)
    all_to_all x1, waiting for transfers between devices, exchange(): lax.all_to_all(x, 'expert', split_axis=0, concat_axis=0, axis_index_group...  67.7 us
    all_to_all x1, blocking collectives, local(): lax.all_to_all(call(count_kernel, shape((devices, WIDE, LANES), jnp.int32...  20.2 us
    ppermute x2, waiting for transfers between devices, along_section(): return lax.ppermute(x, 'section', [(i, (i + by) % n) for i in range(n)])  12 us
    all_to_all x1, starting transfers between devices, exchange(): lax.all_to_all(x, 'expert', split_axis=0, concat_axis=0, axis_index_group...  11.5 us
    pallas_call x1, Pallas kernels, local(): call(functools.partial(finish_kernel, cap), shape((experts, tokens), f32)...  5.05 us
    pallas_call x1, Pallas kernels, local(): call(functools.partial(slab_kernel, cap), shape((PARTS, experts * cap, qu...  4.32 us
  transfers between devices with their start and end apart: 3, of which 2 were waited for; matrix products, arithmetic and copies ran while one was open for 0% of the time, Pallas kernels for 0%

profile of v2, /device:TPU:162, one launch (start us, length us, event | category | flops | bytes accessed | tf_op | source)
XLA Modules:
  0.0 125.1 jit_solution(1966237295500673132)
XLA Ops:
  0.0 1.4 %shard_map.55 = s32[64,2,128]{2,1,0:T(2,128)} custom-call(s32[2,128]{1,0:T(2,128)} %bitcast.21), custom_call_target="tpu_custom_call" | custom-call | bytes 1048576 | tf_op jit(solution)/shard_map/pallas_call | solution.py:158
  1.4 20.2 %all_to_all.10.counts_ref = s32[64,2,128]{2,1,0:T(2,128)} all-to-all(s32[64,2,128]{2,1,0:T(2,128)} %shard_map.55), channel_id=1, replica_groups=mesh['section'=8,'expert'=64] {'expert'}, dimensions={0} | all-to-all | bytes 131072 | tf_op jit(solution)/shard_map/all_to_all | solution.py:157
  21.6 4.3 %shard_map.56 = bf16[4,384,1024]{2,1,0:T(8,128)(2,1)} custom-call(s32[64,2,128]{2,1,0:T(2,128)} %all_to_all.10.counts_ref, bf16[1536,1024]{1,0:T(8,128)(2,1)} %bitcast.19), custom_call_target="tpu_custom_call" | custom-call | bytes 6291456 | tf_op jit(solution)/shard_map/pallas_call | solution.py:161
  25.9 0.0 copy-start.1
  26.0 11.5 %all-to-all-start.1 = ((bf16[64,24,1024]{2,1,0:T(8,128)(2,1)}), bf16[64,24,1024]{2,1,0:T(8,128)(2,1)S(1)}, u32[]{:S(2)}, u32[]{:S(2)}) async-start(bf16[64,24,1024]{2,1,0:T(8,128)(2,1)} %bitcast.18), calls=%async_computation.1 | async-start | bytes 6291456 | tf_op jit(solution)/shard_map/all_to_all | solution.py:28
  37.4 0.0 collective-permute-start.1
  37.5 0.0 copy-done.1
  37.5 0.6 collective-permute-start
  38.1 12.0 %collective-permute-done = bf16[128]{0:T(256)(128)(2,1)S(1)} collective-permute-done((bf16[128]{0:T(256)(128)(2,1)S(1)}, bf16[128]{0:T(256)(128)(2,1)S(1)}, u32[]{:S(2)}, u32[]{:S(2)}) %collective-permute-start) | collective-permute-done | bytes 288 | tf_op jit(solution)/shard_map/ppermute | solution.py:22
  50.1 0.5 bitcast_convert_fusion.scales_ref
  50.6 0.0 collective-permute-done.1.codes_ref
  50.6 67.7 %all-to-all-done.1 = bf16[64,24,1024]{2,1,0:T(8,128)(2,1)S(1)} async-done(((bf16[64,24,1024]{2,1,0:T(8,128)(2,1)}), bf16[64,24,1024]{2,1,0:T(8,128)(2,1)S(1)}, u32[]{:S(2)}, u32[]{:S(2)}) %all-to-all-start.1) | async-done | bytes 3145760 | tf_op jit(solution)/shard_map/all_to_all | solution.py:28
  118.4 0.0 copy-start
  118.4 1.7 %copy-done = bf16[64,24,1024]{2,1,0:T(8,128)(2,1)} copy-done((bf16[64,24,1024]{2,1,0:T(8,128)(2,1)}, bf16[64,24,1024]{2,1,0:T(8,128)(2,1)S(1)}, u32[]{:S(2)}) %copy-start) | copy-done | bytes 3145752
  120.0 5.0 %shard_map.57 = f32[16,128]{1,0:T(8,128)} custom-call(s32[2,128]{1,0:T(2,128)} %bitcast.22, f32[1,128]{1,0:T(1,128)} %bitcast_convert_fusion.scales_ref, f32[16,128]{1,0:T(8,128)} %bitcast.20, bf16[128,4096]{1,0:T(8,128)(2,1)} %collective-permute-done.1.codes_ref, bf16[4,384,1024]{2,1,0:T(8,128)(2,1)} %bitcast.17), custom_call_target="tpu_custom_call" | custom-call | bytes 1048576 | tf_op jit(solution)/shard_map/pallas_call | solution.py:172
Async XLA Ops:
  25.9 11.5 %copy-start.1 = (bf16[1,128]{1,0:T(2,128)(2,1)S(1)}, bf16[1,128]{1,0:T(2,128)(2,1)}, u32[]{:S(2)}) copy-start(bf16[1,128]{1,0:T(2,128)(2,1)} %param.6) | copy-start | bytes 772
  26.0 92.4 %all-to-all-start.1 = ((bf16[64,24,1024]{2,1,0:T(8,128)(2,1)}), bf16[64,24,1024]{2,1,0:T(8,128)(2,1)S(1)}, u32[]{:S(2)}, u32[]{:S(2)}) async-start(bf16[64,24,1024]{2,1,0:T(8,128)(2,1)} %bitcast.18), calls=%async_computation.1 | async-start | bytes 6291456 | tf_op jit(solution)/shard_map/all_to_all | solution.py:28
  37.4 13.2 %collective-permute-start.1 = (bf16[128,4096]{1,0:T(8,128)(2,1)}, bf16[128,4096]{1,0:T(8,128)(2,1)}, u32[]{:S(2)}, u32[]{:S(2)}) collective-permute-start(bf16[128,4096]{1,0:T(8,128)(2,1)} %bitcast.23), channel_id=1, source_target_pairs={{0,448},{64,0},{128,64},{192,128},{256,192},{320,256},{384,320},{4... | collective-permute-start | bytes 3145736 | tf_op jit(solution)/shard_map/ppermute | solution.py:22
  37.5 12.6 %collective-permute-start = (bf16[128]{0:T(256)(128)(2,1)S(1)}, bf16[128]{0:T(256)(128)(2,1)S(1)}, u32[]{:S(2)}, u32[]{:S(2)}) collective-permute-start(bf16[128]{0:T(256)(128)(2,1)S(1)} %bitcast.24), channel_id=1, source_target_pairs={{0,448},{64,0},{128,64},{192,128},{256,192},{320,256},{384,320},{4... | collective-permute-start | bytes 776 | tf_op jit(solution)/shard_map/ppermute | solution.py:22
  118.4 1.7 %copy-start = (bf16[64,24,1024]{2,1,0:T(8,128)(2,1)}, bf16[64,24,1024]{2,1,0:T(8,128)(2,1)S(1)}, u32[]{:S(2)}) copy-start(bf16[64,24,1024]{2,1,0:T(8,128)(2,1)S(1)} %all-to-all-done.1) | copy-start | bytes 9437188

commit v3 on v2

--- a/solution.py
+++ b/solution.py
@@ -10,7 +10,7 @@
 ROWS = 8
 COLS = 8
 PARTS = 4
-WIDE = 2
+WIDE = 1
 LANES = 128
 VMEM = pl.BlockSpec(memory_space=pltpu.VMEM)
 SMEM = pl.BlockSpec(memory_space=pltpu.SMEM)
@@ -30,13 +30,13 @@
     )
 
 
-def call(kernel, out_shape, in_specs, out_specs=None, flops=0, mib=1, **kw):
+def call(kernel, out_shape, in_specs, out_specs=None, flops=0, mib=1, vmem=60, **kw):
     return pl.pallas_call(
         kernel,
         out_shape=out_shape,
         in_specs=in_specs,
         out_specs=jax.tree.map(lambda _: VMEM, out_shape) if out_specs is None else out_specs,
-        compiler_params=pltpu.CompilerParams(vmem_limit_bytes=60 * 1024 * 1024),
+        compiler_params=pltpu.CompilerParams(vmem_limit_bytes=vmem << 20),
         cost_estimate=pl.CostEstimate(flops=flops, bytes_accessed=mib << 20, transcendentals=0),
         **kw,
     )
@@ -59,10 +59,10 @@
         jnp.int32, (devices, devices), 0
     )
     offsets = jnp.dot(
-        earlier.astype(jnp.float32), counts, preferred_element_type=jnp.float32,
-        precision=lax.Precision.HIGHEST,
+        earlier.astype(jnp.bfloat16), counts.astype(jnp.bfloat16),
+        preferred_element_type=jnp.float32,
     ).astype(jnp.int32)
-    at = [jnp.max(offsets[d : d + 1]) for d in range(devices)]
+    at = [offsets[d, 0] for d in range(devices)]
     bases, fetch = [], []
     for r in range(ROWS):
         base = jnp.minimum((at[r * COLS] // 16) * 16, total - reach)
@@ -101,12 +101,9 @@
         w.wait()
 
 
-def finish_kernel(cap, routes_ref, scales_ref, logits_ref, codes_ref, rows_ref, out_ref, rows, sems):
+def finish_kernel(cap, routes_ref, scales_ref, logits_ref, codes_ref, rows, out_ref):
     experts, tokens = logits_ref.shape
     quarter = rows.shape[2]
-    fetch = [pltpu.make_async_copy(rows_ref.at[q], rows.at[q], sems.at[q]) for q in range(PARTS)]
-    for f in fetch:
-        f.start()
     ids = lax.broadcasted_iota(jnp.int32, (experts, tokens), 0)
     hit = (routes_ref[0:1] == ids) | (routes_ref[1:2] == ids)
     upper = lax.broadcasted_iota(jnp.int32, (tokens, tokens), 0) < lax.broadcasted_iota(
@@ -121,7 +118,6 @@
     probs = powers / jnp.sum(powers, axis=0, keepdims=True)
     scores = jnp.zeros((experts * cap, tokens), jnp.float32)
     for q in range(PARTS):
-        fetch[q].wait()
         scores = scores + lax.dot_general(
             rows[q], codes_ref[:, q * quarter : (q + 1) * quarter], (((1,), (1,)), ((), ())),
             preferred_element_type=jnp.float32,
@@ -170,8 +166,7 @@
     )(load, saved)
     rows = exchange(mine.reshape(devices, cap, quarter)).reshape(PARTS, experts * cap, quarter)
     logit_grad = call(
-        functools.partial(finish_kernel, cap), shape((experts, tokens), f32), [VMEM] * 4 + [HBM],
-        scratch_shapes=[pltpu.VMEM((PARTS, experts * cap, quarter), bf16), dma((PARTS,))],
+        functools.partial(finish_kernel, cap), shape((experts, tokens), f32), [VMEM] * 5, vmem=16,
     )(chosen, scales.astype(f32)[None], router_logits[0].T, codes, rows)
     return logit_grad.T[None]
 

time: 125 us -> 121 us (0.968)
  Pallas kernels: 10.8 us -> 7.11 us
    pallas_call x1, Pallas kernels: 5.05 us -> 1.59 us  [local(): call(functools.partial(finish_kernel, cap), shape((experts, tokens), f32)...]
where the time goes in v3:
time: 121 us; the launch traced here: 120 us
  waiting for transfers between devices  78.5 us (65%)
  blocking collectives  20.2 us (17%)
  starting transfers between devices  12 us (10%)
  Pallas kernels  7.11 us (6%)
  local copies, waits for them, and re-layouts  2.23 us (2%)
    all_to_all x1, waiting for transfers between devices, exchange(): lax.all_to_all(x, 'expert', split_axis=0, concat_axis=0, axis_index_group...  66.5 us
    all_to_all x1, blocking collectives, local(): lax.all_to_all(call(count_kernel, shape((devices, WIDE, LANES), jnp.int32...  20.2 us
    ppermute x2, waiting for transfers between devices, along_section(): return lax.ppermute(x, 'section', [(i, (i + by) % n) for i in range(n)])  12 us
    all_to_all x1, starting transfers between devices, exchange(): lax.all_to_all(x, 'expert', split_axis=0, concat_axis=0, axis_index_group...  11.4 us
    pallas_call x1, Pallas kernels, local(): call(functools.partial(slab_kernel, cap), shape((PARTS, experts * cap, qu...  4.14 us
  transfers between devices with their start and end apart: 3, of which 2 were waited for; matrix products, arithmetic and copies ran while one was open for 0% of the time, Pallas kernels for 0%

profile of v3, /device:TPU:162, one launch (start us, length us, event | category | flops | bytes accessed | tf_op | source)
XLA Modules:
  0.0 120.1 jit_solution(8415879698535437760)
XLA Ops:
  0.0 1.4 %shard_map.55 = s32[64,1,128]{2,1,0:T(1,128)} custom-call(s32[2,128]{1,0:T(2,128)} %bitcast.19), custom_call_target="tpu_custom_call" | custom-call | bytes 1048576 | tf_op jit(solution)/shard_map/pallas_call | solution.py:154
  1.4 20.2 %all_to_all.10.counts_ref = s32[64,1,128]{2,1,0:T(1,128)} all-to-all(s32[64,1,128]{2,1,0:T(1,128)} %shard_map.55), channel_id=1, replica_groups=mesh['section'=8,'expert'=64] {'expert'}, dimensions={0} | all-to-all | bytes 65536 | tf_op jit(solution)/shard_map/all_to_all | solution.py:153
  21.6 4.1 %shard_map.56 = bf16[4,384,1024]{2,1,0:T(8,128)(2,1)} custom-call(s32[64,1,128]{2,1,0:T(1,128)} %all_to_all.10.counts_ref, bf16[1536,1024]{1,0:T(8,128)(2,1)} %bitcast.22), custom_call_target="tpu_custom_call" | custom-call | bytes 6291456 | tf_op jit(solution)/shard_map/pallas_call | solution.py:157
  25.7 0.0 copy-start.4
  25.8 0.0 copy-start.2
  25.8 0.0 copy-start.3
  25.8 11.4 %all-to-all-start.1 = ((bf16[64,24,1024]{2,1,0:T(8,128)(2,1)}), bf16[64,24,1024]{2,1,0:T(8,128)(2,1)S(1)}, u32[]{:S(2)}, u32[]{:S(2)}) async-start(bf16[64,24,1024]{2,1,0:T(8,128)(2,1)} %bitcast.21), calls=%async_computation.1 | async-start | bytes 6291456 | tf_op jit(solution)/shard_map/all_to_all | solution.py:28
  37.2 0.0 collective-permute-start.1
  37.2 0.0 copy-done.4
  37.2 0.6 collective-permute-start
  37.8 12.0 %collective-permute-done = bf16[128]{0:T(256)(128)(2,1)S(1)} collective-permute-done((bf16[128]{0:T(256)(128)(2,1)S(1)}, bf16[128]{0:T(256)(128)(2,1)S(1)}, u32[]{:S(2)}, u32[]{:S(2)}) %collective-permute-start) | collective-permute-done | bytes 288 | tf_op jit(solution)/shard_map/ppermute | solution.py:22
  49.8 0.0 collective-permute-done.1.codes_ref
  49.8 0.0 copy-start
  49.8 1.0 copy-done
  50.8 66.5 %all-to-all-done.1 = bf16[64,24,1024]{2,1,0:T(8,128)(2,1)S(1)} async-done(((bf16[64,24,1024]{2,1,0:T(8,128)(2,1)}), bf16[64,24,1024]{2,1,0:T(8,128)(2,1)S(1)}, u32[]{:S(2)}, u32[]{:S(2)}) %all-to-all-start.1) | async-done | bytes 3145760 | tf_op jit(solution)/shard_map/all_to_all | solution.py:28
  117.3 0.0 copy-done.2
  117.3 0.0 copy-done.3
  117.3 0.0 copy-start.1
  117.3 1.2 %copy-done.1 = bf16[128,4096]{1,0:T(8,128)(2,1)S(1)} copy-done((bf16[128,4096]{1,0:T(8,128)(2,1)S(1)}, bf16[128,4096]{1,0:T(8,128)(2,1)}, u32[]{:S(2)}) %copy-start.1) | copy-done | bytes 1048600
  118.6 1.6 %shard_map.57 = f32[16,128]{1,0:T(8,128)} custom-call(s32[2,128]{1,0:T(2,128)S(1)} %bitcast.20, f32[1,128]{1,0:T(1,128)S(1)} %bitcast_convert_fusion.scales_ref, f32[16,128]{1,0:T(8,128)S(1)} %bitcast.18, bf16[128,4096]{1,0:T(8,128)(2,1)S(1)} %copy-done.1, bf16[4,384,1024]{2,1,0:T(8,128)(2,1)S(1)} %bitcast.17), custom_call_target="tpu_custom_call" | custom-call | bytes 1048576 | tf_op jit(solution)/shard_map/pallas_call | solution.py:168
  (1 shorter events, 0.0 us)
Async XLA Ops:
  25.7 11.5 %copy-start.4 = (bf16[1,128]{1,0:T(2,128)(2,1)S(1)}, bf16[1,128]{1,0:T(2,128)(2,1)}, u32[]{:S(2)}) copy-start(bf16[1,128]{1,0:T(2,128)(2,1)} %param.6) | copy-start | bytes 772
  25.8 91.6 %copy-start.2 = (f32[1,128,16]{1,2,0:T(8,128)S(1)}, f32[1,128,16]{1,2,0:T(8,128)}, u32[]{:S(2)}) copy-start(f32[1,128,16]{1,2,0:T(8,128)} %param.8) | copy-start | bytes 24580
  25.8 91.6 %copy-start.3 = (s32[1,128,2]{1,2,0:T(2,128)S(1)}, s32[1,128,2]{1,2,0:T(2,128)}, u32[]{:S(2)}) copy-start(s32[1,128,2]{1,2,0:T(2,128)} %param.7) | copy-start | bytes 3076
  25.8 91.5 %all-to-all-start.1 = ((bf16[64,24,1024]{2,1,0:T(8,128)(2,1)}), bf16[64,24,1024]{2,1,0:T(8,128)(2,1)S(1)}, u32[]{:S(2)}, u32[]{:S(2)}) async-start(bf16[64,24,1024]{2,1,0:T(8,128)(2,1)} %bitcast.21), calls=%async_computation.1 | async-start | bytes 6291456 | tf_op jit(solution)/shard_map/all_to_all | solution.py:28
  37.2 12.7 %collective-permute-start.1 = (bf16[128,4096]{1,0:T(8,128)(2,1)}, bf16[128,4096]{1,0:T(8,128)(2,1)S(1)}, u32[]{:S(2)}, u32[]{:S(2)}) collective-permute-start(bf16[128,4096]{1,0:T(8,128)(2,1)} %bitcast.23), channel_id=1, source_target_pairs={{0,448},{64,0},{128,64},{192,128},{256,192},{320,256},{384,320},{4... | collective-permute-start | bytes 3145736 | tf_op jit(solution)/shard_map/ppermute | solution.py:22
  37.2 12.6 %collective-permute-start = (bf16[128]{0:T(256)(128)(2,1)S(1)}, bf16[128]{0:T(256)(128)(2,1)S(1)}, u32[]{:S(2)}, u32[]{:S(2)}) collective-permute-start(bf16[128]{0:T(256)(128)(2,1)S(1)} %bitcast.24), channel_id=1, source_target_pairs={{0,448},{64,0},{128,64},{192,128},{256,192},{320,256},{384,320},{4... | collective-permute-start | bytes 776 | tf_op jit(solution)/shard_map/ppermute | solution.py:22
  49.8 1.0 copy-start
  117.3 1.2 %copy-start.1 = (bf16[128,4096]{1,0:T(8,128)(2,1)S(1)}, bf16[128,4096]{1,0:T(8,128)(2,1)}, u32[]{:S(2)}) copy-start(bf16[128,4096]{1,0:T(8,128)(2,1)} %copy-done) | copy-start | bytes 3145732

commit v4 on v3

--- a/solution.py
+++ b/solution.py
@@ -51,10 +51,22 @@
         out_ref[o] = jnp.broadcast_to(counts[o // PARTS : o // PARTS + 1], (WIDE, LANES))
 
 
-def slab_kernel(cap, counts_ref, saved_ref, out_ref, windows, wide, slabs, reads, writes):
+def slab_kernel(cap, counts_ref, saved_ref, out_ref, held, counts_vmem, wide, slabs, reads, writes):
     devices = ROWS * COLS
-    total, reach, tail = saved_ref.shape[0], windows.shape[1], wide.shape[2]
-    counts = counts_ref[:, 0].astype(jnp.float32)
+    total, tail = saved_ref.shape[0], wide.shape[2]
+    reach, depth = tail - cap, total // ROWS
+    first = pltpu.make_async_copy(counts_ref, counts_vmem, reads.at[ROWS])
+    first.start()
+    fetch = [
+        pltpu.make_async_copy(
+            saved_ref.at[pl.ds(r * depth, depth)], held.at[pl.ds(r * depth, depth)], reads.at[r]
+        )
+        for r in range(ROWS)
+    ]
+    for f in fetch:
+        f.start()
+    first.wait()
+    counts = counts_vmem[:, 0].astype(jnp.float32)
     earlier = lax.broadcasted_iota(jnp.int32, (devices, devices), 1) < lax.broadcasted_iota(
         jnp.int32, (devices, devices), 0
     )
@@ -63,16 +75,10 @@
         preferred_element_type=jnp.float32,
     ).astype(jnp.int32)
     at = [offsets[d, 0] for d in range(devices)]
-    bases, fetch = [], []
-    for r in range(ROWS):
-        base = jnp.minimum((at[r * COLS] // 16) * 16, total - reach)
-        bases.append(pl.multiple_of(base, 16))
-        fetch.append(
-            pltpu.make_async_copy(
-                saved_ref.at[pl.ds(bases[r], reach)], windows.at[r], reads.at[r]
-            )
-        )
-        fetch[r].start()
+    bases = [
+        pl.multiple_of(jnp.minimum((at[r * COLS] // 16) * 16, total - reach), 16)
+        for r in range(ROWS)
+    ]
     for b in range(2):
         wide[b, :, reach:] = jnp.zeros((wide.shape[1], tail - reach, LANES), jnp.float32)
     two = 2 * cap
@@ -84,9 +90,12 @@
     ]
     for r in range(ROWS):
         b = r % 2
-        fetch[r].wait()
+        for f in fetch[:2] if r == 0 else fetch[r + 1 : r + 2]:
+            f.wait()
         for k in range(wide.shape[1]):
-            wide[b, k, :reach] = windows[r, :, k * LANES : (k + 1) * LANES].astype(jnp.float32)
+            wide[b, k, :reach] = held[
+                pl.ds(bases[r], reach), k * LANES : (k + 1) * LANES
+            ].astype(jnp.float32)
         for k in range(wide.shape[1]):
             for q in range(PARTS):
                 rows = [
@@ -156,12 +165,13 @@
     )
     mine = call(
         functools.partial(slab_kernel, cap), shape((PARTS, experts * cap, quarter), bf16),
-        [VMEM, HBM], HBM, mib=6,
+        [HBM, HBM], HBM, mib=6,
         scratch_shapes=[
-            pltpu.VMEM((ROWS, slab + 16, quarter), bf16),
+            pltpu.VMEM(saved.shape, bf16),
+            pltpu.VMEM((devices, WIDE, LANES), jnp.int32),
             pltpu.VMEM((2, quarter // LANES, slab + 16 + cap, LANES), f32),
             pltpu.VMEM((PARTS, experts * cap, quarter), bf16),
-            dma((ROWS,)), dma((ROWS,)),
+            dma((ROWS + 1,)), dma((ROWS,)),
         ],
     )(load, saved)
     rows = exchange(mine.reshape(devices, cap, quarter)).reshape(PARTS, experts * cap, quarter)

time: 121 us -> 120 us (level)
  the two profiles are of different devices: /device:TPU:162 before, /device:TPU:160 now
where the time goes in v4:
time: 120 us; the launch traced here: 119 us
  waiting for transfers between devices  76.3 us (64%)
  blocking collectives  20.2 us (17%)
  starting transfers between devices  14.3 us (12%)
  Pallas kernels  6.26 us (5%)
  local copies, waits for them, and re-layouts  2.23 us (2%)
    all_to_all x1, waiting for transfers between devices, exchange(): lax.all_to_all(x, 'expert', split_axis=0, concat_axis=0, axis_index_group...  66.2 us
    all_to_all x1, blocking collectives, local(): lax.all_to_all(call(count_kernel, shape((devices, WIDE, LANES), jnp.int32...  20.2 us
    all_to_all x1, starting transfers between devices, exchange(): lax.all_to_all(x, 'expert', split_axis=0, concat_axis=0, axis_index_group...  11.4 us
    ppermute x2, waiting for transfers between devices, along_section(): return lax.ppermute(x, 'section', [(i, (i + by) % n) for i in range(n)])  10.1 us
    pallas_call x1, Pallas kernels, local(): call(functools.partial(slab_kernel, cap), shape((PARTS, experts * cap, qu...  3.29 us
    ppermute x2, starting transfers between devices, along_section(): return lax.ppermute(x, 'section', [(i, (i + by) % n) for i in range(n)])  2.88 us
  transfers between devices with their start and end apart: 3, of which 2 were waited for; matrix products, arithmetic and copies ran while one was open for 0% of the time, Pallas kernels for 0%

profile of v4, /device:TPU:160, one launch (start us, length us, event | category | flops | bytes accessed | tf_op | source)
XLA Modules:
  0.0 119.4 jit_solution(8023811713541869406)
XLA Ops:
  0.0 1.4 %shard_map.55 = s32[64,1,128]{2,1,0:T(1,128)} custom-call(s32[2,128]{1,0:T(2,128)} %bitcast.19), custom_call_target="tpu_custom_call" | custom-call | bytes 1048576 | tf_op jit(solution)/shard_map/pallas_call | solution.py:163
  1.4 20.2 %all_to_all.10.counts_ref = s32[64,1,128]{2,1,0:T(1,128)} all-to-all(s32[64,1,128]{2,1,0:T(1,128)} %shard_map.55), channel_id=1, replica_groups=mesh['section'=8,'expert'=64] {'expert'}, dimensions={0} | all-to-all | bytes 65536 | tf_op jit(solution)/shard_map/all_to_all | solution.py:162
  21.6 3.3 %shard_map.56 = bf16[4,384,1024]{2,1,0:T(8,128)(2,1)} custom-call(s32[64,1,128]{2,1,0:T(1,128)} %all_to_all.10.counts_ref, bf16[1536,1024]{1,0:T(8,128)(2,1)} %bitcast.22), custom_call_target="tpu_custom_call" | custom-call | bytes 6291456 | tf_op jit(solution)/shard_map/pallas_call | solution.py:166
  24.9 0.0 copy-start.4
  24.9 0.0 copy-start.2
  24.9 0.0 copy-start.3
  24.9 11.4 %all-to-all-start.1 = ((bf16[64,24,1024]{2,1,0:T(8,128)(2,1)}), bf16[64,24,1024]{2,1,0:T(8,128)(2,1)S(1)}, u32[]{:S(2)}, u32[]{:S(2)}) async-start(bf16[64,24,1024]{2,1,0:T(8,128)(2,1)} %bitcast.21), calls=%async_computation.1 | async-start | bytes 6291456 | tf_op jit(solution)/shard_map/all_to_all | solution.py:28
  36.3 0.4 collective-permute-start.1
  36.7 0.0 copy-done.4
  36.7 2.5 %collective-permute-start = (bf16[128]{0:T(256)(128)(2,1)S(1)}, bf16[128]{0:T(256)(128)(2,1)S(1)}, u32[]{:S(2)}, u32[]{:S(2)}) collective-permute-start(bf16[128]{0:T(256)(128)(2,1)S(1)} %bitcast.24), channel_id=1, source_target_pairs={{0,448},{64,0},{128,64},{192,128},{256,192},{320,256},{384,320},{4... | collective-permute-start | bytes 776 | tf_op jit(solution)/shard_map/ppermute | solution.py:22
  39.2 10.1 %collective-permute-done = bf16[128]{0:T(256)(128)(2,1)S(1)} collective-permute-done((bf16[128]{0:T(256)(128)(2,1)S(1)}, bf16[128]{0:T(256)(128)(2,1)S(1)}, u32[]{:S(2)}, u32[]{:S(2)}) %collective-permute-start) | collective-permute-done | bytes 288 | tf_op jit(solution)/shard_map/ppermute | solution.py:22
  49.3 0.0 collective-permute-done.1.codes_ref
  49.3 0.0 copy-start
  49.3 1.0 copy-done
  50.3 66.2 %all-to-all-done.1 = bf16[64,24,1024]{2,1,0:T(8,128)(2,1)S(1)} async-done(((bf16[64,24,1024]{2,1,0:T(8,128)(2,1)}), bf16[64,24,1024]{2,1,0:T(8,128)(2,1)S(1)}, u32[]{:S(2)}, u32[]{:S(2)}) %all-to-all-start.1) | async-done | bytes 3145760 | tf_op jit(solution)/shard_map/all_to_all | solution.py:28
  116.5 0.0 copy-done.2
  116.5 0.0 copy-done.3
  116.5 0.0 copy-start.1
  116.5 1.2 %copy-done.1 = bf16[128,4096]{1,0:T(8,128)(2,1)S(1)} copy-done((bf16[128,4096]{1,0:T(8,128)(2,1)S(1)}, bf16[128,4096]{1,0:T(8,128)(2,1)}, u32[]{:S(2)}) %copy-start.1) | copy-done | bytes 1048600
  117.8 1.6 %shard_map.57 = f32[16,128]{1,0:T(8,128)} custom-call(s32[2,128]{1,0:T(2,128)S(1)} %bitcast.20, f32[1,128]{1,0:T(1,128)S(1)} %bitcast_convert_fusion.scales_ref, f32[16,128]{1,0:T(8,128)S(1)} %bitcast.18, bf16[128,4096]{1,0:T(8,128)(2,1)S(1)} %copy-done.1, bf16[4,384,1024]{2,1,0:T(8,128)(2,1)S(1)} %bitcast.17), custom_call_target="tpu_custom_call" | custom-call | bytes 1048576 | tf_op jit(solution)/shard_map/pallas_call | solution.py:178
  (1 shorter events, 0.0 us)
Async XLA Ops:
  24.9 11.8 %copy-start.4 = (bf16[1,128]{1,0:T(2,128)(2,1)S(1)}, bf16[1,128]{1,0:T(2,128)(2,1)}, u32[]{:S(2)}) copy-start(bf16[1,128]{1,0:T(2,128)(2,1)} %param.6) | copy-start | bytes 772
  24.9 91.6 %copy-start.2 = (f32[1,128,16]{1,2,0:T(8,128)S(1)}, f32[1,128,16]{1,2,0:T(8,128)}, u32[]{:S(2)}) copy-start(f32[1,128,16]{1,2,0:T(8,128)} %param.8) | copy-start | bytes 24580
  24.9 91.6 %copy-start.3 = (s32[1,128,2]{1,2,0:T(2,128)S(1)}, s32[1,128,2]{1,2,0:T(2,128)}, u32[]{:S(2)}) copy-start(s32[1,128,2]{1,2,0:T(2,128)} %param.7) | copy-start | bytes 3076
  24.9 91.6 %all-to-all-start.1 = ((bf16[64,24,1024]{2,1,0:T(8,128)(2,1)}), bf16[64,24,1024]{2,1,0:T(8,128)(2,1)S(1)}, u32[]{:S(2)}, u32[]{:S(2)}) async-start(bf16[64,24,1024]{2,1,0:T(8,128)(2,1)} %bitcast.21), calls=%async_computation.1 | async-start | bytes 6291456 | tf_op jit(solution)/shard_map/all_to_all | solution.py:28
  36.3 13.0 %collective-permute-start.1 = (bf16[128,4096]{1,0:T(8,128)(2,1)}, bf16[128,4096]{1,0:T(8,128)(2,1)S(1)}, u32[]{:S(2)}, u32[]{:S(2)}) collective-permute-start(bf16[128,4096]{1,0:T(8,128)(2,1)} %bitcast.23), channel_id=1, source_target_pairs={{0,448},{64,0},{128,64},{192,128},{256,192},{320,256},{384,320},{4... | collective-permute-start | bytes 3145736 | tf_op jit(solution)/shard_map/ppermute | solution.py:22
  36.7 12.6 %collective-permute-start = (bf16[128]{0:T(256)(128)(2,1)S(1)}, bf16[128]{0:T(256)(128)(2,1)S(1)}, u32[]{:S(2)}, u32[]{:S(2)}) collective-permute-start(bf16[128]{0:T(256)(128)(2,1)S(1)} %bitcast.24), channel_id=1, source_target_pairs={{0,448},{64,0},{128,64},{192,128},{256,192},{320,256},{384,320},{4... | collective-permute-start | bytes 776 | tf_op jit(solution)/shard_map/ppermute | solution.py:22
  49.3 1.0 copy-start
  116.5 1.2 %copy-start.1 = (bf16[128,4096]{1,0:T(8,128)(2,1)S(1)}, bf16[128,4096]{1,0:T(8,128)(2,1)}, u32[]{:S(2)}) copy-start(bf16[128,4096]{1,0:T(8,128)(2,1)} %copy-done) | copy-start | bytes 3145732

commit v5 on v4

--- a/solution.py
+++ b/solution.py
@@ -10,6 +10,7 @@
 ROWS = 8
 COLS = 8
 PARTS = 4
+PART_AT = (0, 2, 1, 3)
 WIDE = 1
 LANES = 128
 VMEM = pl.BlockSpec(memory_space=pltpu.VMEM)
@@ -24,7 +25,7 @@
 
 def exchange(x):
     devices = ROWS * COLS
-    order = [i * PARTS + q for q in range(PARTS) for i in range(devices // PARTS)]
+    order = [i * PARTS + q for q in PART_AT for i in range(devices // PARTS)]
     return lax.all_to_all(
         x, "expert", split_axis=0, concat_axis=0, axis_index_groups=[order], tiled=True
     )
@@ -102,7 +103,7 @@
                     wide[b, k, pl.ds(at[r * COLS + c] - bases[r], cap), :]
                     for c in (q, q + PARTS)
                 ]
-                slabs[q, r * two : (r + 1) * two, k * LANES : (k + 1) * LANES] = jnp.concatenate(
+                slabs[PART_AT[q], r * two : (r + 1) * two, k * LANES : (k + 1) * LANES] = jnp.concatenate(
                     rows, axis=0
                 ).astype(jnp.bfloat16)
         store[r].start()
@@ -128,7 +129,7 @@
     scores = jnp.zeros((experts * cap, tokens), jnp.float32)
     for q in range(PARTS):
         scores = scores + lax.dot_general(
-            rows[q], codes_ref[:, q * quarter : (q + 1) * quarter], (((1,), (1,)), ((), ())),
+            rows[PART_AT[q]], codes_ref[:, q * quarter : (q + 1) * quarter], (((1,), (1,)), ((), ())),
             preferred_element_type=jnp.float32,
         )
     line = lax.broadcasted_iota(jnp.int32, (cap, tokens), 0).astype(jnp.float32)

time: 120 us -> 117 us (0.975)
  the two profiles are of different devices: /device:TPU:160 before, /device:TPU:6 now
where the time goes in v5:
time: 117 us; the launch traced here: 115 us
  waiting for transfers between devices  72.3 us (62%)
  blocking collectives  28.7 us (25%)
  Pallas kernels  6.26 us (5%)
  starting transfers between devices  5.82 us (5%)
  local copies, waits for them, and re-layouts  2.23 us (2%)
    all_to_all x1, waiting for transfers between devices, exchange(): lax.all_to_all(x, 'expert', split_axis=0, concat_axis=0, axis_index_group...  60.6 us
    all_to_all x1, blocking collectives, local(): lax.all_to_all(call(count_kernel, shape((devices, WIDE, LANES), jnp.int32...  28.7 us
    ppermute x2, waiting for transfers between devices, along_section(): return lax.ppermute(x, 'section', [(i, (i + by) % n) for i in range(n)])  11.7 us
    all_to_all x1, starting transfers between devices, exchange(): lax.all_to_all(x, 'expert', split_axis=0, concat_axis=0, axis_index_group...  4.88 us
    pallas_call x1, Pallas kernels, local(): call(functools.partial(slab_kernel, cap), shape((PARTS, experts * cap, qu...  3.29 us
  transfers between devices with their start and end apart: 3, of which 2 were waited for; matrix products, arithmetic and copies ran while one was open for 0% of the time, Pallas kernels for 0%

profile of v5, /device:TPU:6, one launch (start us, length us, event | category | flops | bytes accessed | tf_op | source)
XLA Modules:
  0.0 115.4 jit_solution(2770045312314045603)
XLA Ops:
  0.0 1.4 %shard_map.55 = s32[64,1,128]{2,1,0:T(1,128)} custom-call(s32[2,128]{1,0:T(2,128)} %bitcast.19), custom_call_target="tpu_custom_call" | custom-call | bytes 1048576 | tf_op jit(solution)/shard_map/pallas_call | solution.py:164
  1.4 28.7 %all_to_all.10.counts_ref = s32[64,1,128]{2,1,0:T(1,128)} all-to-all(s32[64,1,128]{2,1,0:T(1,128)} %shard_map.55), channel_id=1, replica_groups=mesh['section'=8,'expert'=64] {'expert'}, dimensions={0} | all-to-all | bytes 65536 | tf_op jit(solution)/shard_map/all_to_all | solution.py:163
  30.1 3.3 %shard_map.56 = bf16[4,384,1024]{2,1,0:T(8,128)(2,1)} custom-call(s32[64,1,128]{2,1,0:T(1,128)} %all_to_all.10.counts_ref, bf16[1536,1024]{1,0:T(8,128)(2,1)} %bitcast.22), custom_call_target="tpu_custom_call" | custom-call | bytes 6291456 | tf_op jit(solution)/shard_map/pallas_call | solution.py:167
  33.4 0.0 copy-start.4
  33.4 0.0 copy-start.2
  33.4 0.0 copy-start.3
  33.5 4.9 %all-to-all-start.1 = ((bf16[64,24,1024]{2,1,0:T(8,128)(2,1)}), bf16[64,24,1024]{2,1,0:T(8,128)(2,1)S(1)}, u32[]{:S(2)}, u32[]{:S(2)}) async-start(bf16[64,24,1024]{2,1,0:T(8,128)(2,1)} %bitcast.21), calls=%async_computation.1 | async-start | bytes 6291456 | tf_op jit(solution)/shard_map/all_to_all | solution.py:29
  38.3 0.0 collective-permute-start.1
  38.4 0.0 copy-done.4
  38.4 0.9 collective-permute-start
  39.3 11.7 %collective-permute-done = bf16[128]{0:T(256)(128)(2,1)S(1)} collective-permute-done((bf16[128]{0:T(256)(128)(2,1)S(1)}, bf16[128]{0:T(256)(128)(2,1)S(1)}, u32[]{:S(2)}, u32[]{:S(2)}) %collective-permute-start) | collective-permute-done | bytes 288 | tf_op jit(solution)/shard_map/ppermute | solution.py:23
  51.0 0.0 collective-permute-done.1.codes_ref
  51.0 0.0 copy-start
  51.0 1.0 copy-done
  52.0 60.6 %all-to-all-done.1 = bf16[64,24,1024]{2,1,0:T(8,128)(2,1)S(1)} async-done(((bf16[64,24,1024]{2,1,0:T(8,128)(2,1)}), bf16[64,24,1024]{2,1,0:T(8,128)(2,1)S(1)}, u32[]{:S(2)}, u32[]{:S(2)}) %all-to-all-start.1) | async-done | bytes 3145760 | tf_op jit(solution)/shard_map/all_to_all | solution.py:29
  112.6 0.0 copy-done.2
  112.6 0.0 copy-done.3
  112.6 0.0 copy-start.1
  112.6 1.2 %copy-done.1 = bf16[128,4096]{1,0:T(8,128)(2,1)S(1)} copy-done((bf16[128,4096]{1,0:T(8,128)(2,1)S(1)}, bf16[128,4096]{1,0:T(8,128)(2,1)}, u32[]{:S(2)}) %copy-start.1) | copy-done | bytes 1048600
  113.8 1.6 %shard_map.57 = f32[16,128]{1,0:T(8,128)} custom-call(s32[2,128]{1,0:T(2,128)S(1)} %bitcast.20, f32[1,128]{1,0:T(1,128)S(1)} %bitcast_convert_fusion.scales_ref, f32[16,128]{1,0:T(8,128)S(1)} %bitcast.18, bf16[128,4096]{1,0:T(8,128)(2,1)S(1)} %copy-done.1, bf16[4,384,1024]{2,1,0:T(8,128)(2,1)S(1)} %bitcast.17), custom_call_target="tpu_custom_call" | custom-call | bytes 1048576 | tf_op jit(solution)/shard_map/pallas_call | solution.py:179
  (1 shorter events, 0.0 us)
Async XLA Ops:
  33.4 5.0 %copy-start.4 = (bf16[1,128]{1,0:T(2,128)(2,1)S(1)}, bf16[1,128]{1,0:T(2,128)(2,1)}, u32[]{:S(2)}) copy-start(bf16[1,128]{1,0:T(2,128)(2,1)} %param.6) | copy-start | bytes 772
  33.4 79.2 %copy-start.2 = (f32[1,128,16]{1,2,0:T(8,128)S(1)}, f32[1,128,16]{1,2,0:T(8,128)}, u32[]{:S(2)}) copy-start(f32[1,128,16]{1,2,0:T(8,128)} %param.8) | copy-start | bytes 24580
  33.4 79.2 %copy-start.3 = (s32[1,128,2]{1,2,0:T(2,128)S(1)}, s32[1,128,2]{1,2,0:T(2,128)}, u32[]{:S(2)}) copy-start(s32[1,128,2]{1,2,0:T(2,128)} %param.7) | copy-start | bytes 3076
  33.5 79.1 %all-to-all-start.1 = ((bf16[64,24,1024]{2,1,0:T(8,128)(2,1)}), bf16[64,24,1024]{2,1,0:T(8,128)(2,1)S(1)}, u32[]{:S(2)}, u32[]{:S(2)}) async-start(bf16[64,24,1024]{2,1,0:T(8,128)(2,1)} %bitcast.21), calls=%async_computation.1 | async-start | bytes 6291456 | tf_op jit(solution)/shard_map/all_to_all | solution.py:29
  38.3 12.7 %collective-permute-start.1 = (bf16[128,4096]{1,0:T(8,128)(2,1)}, bf16[128,4096]{1,0:T(8,128)(2,1)S(1)}, u32[]{:S(2)}, u32[]{:S(2)}) collective-permute-start(bf16[128,4096]{1,0:T(8,128)(2,1)} %bitcast.23), channel_id=1, source_target_pairs={{0,448},{64,0},{128,64},{192,128},{256,192},{320,256},{384,320},{4... | collective-permute-start | bytes 3145736 | tf_op jit(solution)/shard_map/ppermute | solution.py:23
  38.4 12.6 %collective-permute-start = (bf16[128]{0:T(256)(128)(2,1)S(1)}, bf16[128]{0:T(256)(128)(2,1)S(1)}, u32[]{:S(2)}, u32[]{:S(2)}) collective-permute-start(bf16[128]{0:T(256)(128)(2,1)S(1)} %bitcast.24), channel_id=1, source_target_pairs={{0,448},{64,0},{128,64},{192,128},{256,192},{320,256},{384,320},{4... | collective-permute-start | bytes 776 | tf_op jit(solution)/shard_map/ppermute | solution.py:23
  51.0 1.0 copy-start
  112.6 1.2 %copy-start.1 = (bf16[128,4096]{1,0:T(8,128)(2,1)S(1)}, bf16[128,4096]{1,0:T(8,128)(2,1)}, u32[]{:S(2)}) copy-start(bf16[128,4096]{1,0:T(8,128)(2,1)} %copy-done) | copy-start | bytes 3145732

commit v6 on v5

--- a/solution.py
+++ b/solution.py
@@ -10,6 +10,7 @@
 ROWS = 8
 COLS = 8
 PARTS = 4
+ROW_AT = (0, 5, 2, 7, 4, 1, 6, 3)
 PART_AT = (0, 2, 1, 3)
 WIDE = 1
 LANES = 128
@@ -25,7 +26,7 @@
 
 def exchange(x):
     devices = ROWS * COLS
-    order = [i * PARTS + q for q in PART_AT for i in range(devices // PARTS)]
+    order = [r * COLS + h * PARTS + q for q in PART_AT for r in ROW_AT for h in range(2)]
     return lax.all_to_all(
         x, "expert", split_axis=0, concat_axis=0, axis_index_groups=[order], tiled=True
     )
@@ -85,7 +86,8 @@
     two = 2 * cap
     store = [
         pltpu.make_async_copy(
-            slabs.at[:, pl.ds(r * two, two)], out_ref.at[:, pl.ds(r * two, two)], writes.at[r]
+            slabs.at[:, pl.ds(ROW_AT[r] * two, two)],
+            out_ref.at[:, pl.ds(ROW_AT[r] * two, two)], writes.at[r]
         )
         for r in range(ROWS)
     ]
@@ -103,7 +105,7 @@
                     wide[b, k, pl.ds(at[r * COLS + c] - bases[r], cap), :]
                     for c in (q, q + PARTS)
                 ]
-                slabs[PART_AT[q], r * two : (r + 1) * two, k * LANES : (k + 1) * LANES] = jnp.concatenate(
+                slabs[PART_AT[q], ROW_AT[r] * two : (ROW_AT[r] + 1) * two, k * LANES : (k + 1) * LANES] = jnp.concatenate(
                     rows, axis=0
                 ).astype(jnp.bfloat16)
         store[r].start()
@@ -133,10 +135,11 @@
             preferred_element_type=jnp.float32,
         )
     line = lax.broadcasted_iota(jnp.int32, (cap, tokens), 0).astype(jnp.float32)
+    at = [(2 * ROW_AT[e // 2] + e % 2) * cap for e in range(experts)]
     gate = jnp.concatenate(
         [
             jnp.sum(
-                jnp.where(line == want[e : e + 1], scores[e * cap : (e + 1) * cap], 0.0),
+                jnp.where(line == want[e : e + 1], scores[at[e] : at[e] + cap], 0.0),
                 axis=0, keepdims=True,
             )
             for e in range(experts)

time: 117 us -> 118 us (level)
  no operation moved by 1% of the time
where the time goes in v6:
time: 118 us; the launch traced here: 116 us
  waiting for transfers between devices  73.1 us (62%)
  blocking collectives  28.7 us (24%)
  Pallas kernels  6.23 us (5%)
  starting transfers between devices  5.82 us (5%)
  local copies, waits for them, and re-layouts  2.23 us (2%)
    all_to_all x1, waiting for transfers between devices, exchange(): lax.all_to_all(x, 'expert', split_axis=0, concat_axis=0, axis_index_group...  61.5 us
    all_to_all x1, blocking collectives, local(): lax.all_to_all(call(count_kernel, shape((devices, WIDE, LANES), jnp.int32...  28.7 us
    ppermute x2, waiting for transfers between devices, along_section(): return lax.ppermute(x, 'section', [(i, (i + by) % n) for i in range(n)])  11.7 us
    all_to_all x1, starting transfers between devices, exchange(): lax.all_to_all(x, 'expert', split_axis=0, concat_axis=0, axis_index_group...  4.88 us
    pallas_call x1, Pallas kernels, local(): call(functools.partial(slab_kernel, cap), shape((PARTS, experts * cap, qu...  3.26 us
  transfers between devices with their start and end apart: 3, of which 2 were waited for; matrix products, arithmetic and copies ran while one was open for 0% of the time, Pallas kernels for 0%

profile of v6, /device:TPU:6, one launch (start us, length us, event | category | flops | bytes accessed | tf_op | source)
XLA Modules:
  0.0 116.2 jit_solution(10843425079207584978)
XLA Ops:
  0.0 1.4 %shard_map.55 = s32[64,1,128]{2,1,0:T(1,128)} custom-call(s32[2,128]{1,0:T(2,128)} %bitcast.19), custom_call_target="tpu_custom_call" | custom-call | bytes 1048576 | tf_op jit(solution)/shard_map/pallas_call | solution.py:167
  1.4 28.7 %all_to_all.10.counts_ref = s32[64,1,128]{2,1,0:T(1,128)} all-to-all(s32[64,1,128]{2,1,0:T(1,128)} %shard_map.55), channel_id=1, replica_groups=mesh['section'=8,'expert'=64] {'expert'}, dimensions={0} | all-to-all | bytes 65536 | tf_op jit(solution)/shard_map/all_to_all | solution.py:166
  30.1 3.3 %shard_map.56 = bf16[4,384,1024]{2,1,0:T(8,128)(2,1)} custom-call(s32[64,1,128]{2,1,0:T(1,128)} %all_to_all.10.counts_ref, bf16[1536,1024]{1,0:T(8,128)(2,1)} %bitcast.22), custom_call_target="tpu_custom_call" | custom-call | bytes 6291456 | tf_op jit(solution)/shard_map/pallas_call | solution.py:170
  33.4 0.0 copy-start.4
  33.4 0.0 copy-start.2
  33.4 0.0 copy-start.3
  33.4 4.9 %all-to-all-start.1 = ((bf16[64,24,1024]{2,1,0:T(8,128)(2,1)}), bf16[64,24,1024]{2,1,0:T(8,128)(2,1)S(1)}, u32[]{:S(2)}, u32[]{:S(2)}) async-start(bf16[64,24,1024]{2,1,0:T(8,128)(2,1)} %bitcast.21), calls=%async_computation.1 | async-start | bytes 6291456 | tf_op jit(solution)/shard_map/all_to_all | solution.py:30
  38.3 0.0 collective-permute-start.1
  38.3 0.0 copy-done.4
  38.3 0.9 collective-permute-start
  39.3 11.7 %collective-permute-done = bf16[128]{0:T(256)(128)(2,1)S(1)} collective-permute-done((bf16[128]{0:T(256)(128)(2,1)S(1)}, bf16[128]{0:T(256)(128)(2,1)S(1)}, u32[]{:S(2)}, u32[]{:S(2)}) %collective-permute-start) | collective-permute-done | bytes 288 | tf_op jit(solution)/shard_map/ppermute | solution.py:24
  51.0 0.0 collective-permute-done.1.codes_ref
  51.0 0.0 copy-start
  51.0 1.0 copy-done
  52.0 61.5 %all-to-all-done.1 = bf16[64,24,1024]{2,1,0:T(8,128)(2,1)S(1)} async-done(((bf16[64,24,1024]{2,1,0:T(8,128)(2,1)}), bf16[64,24,1024]{2,1,0:T(8,128)(2,1)S(1)}, u32[]{:S(2)}, u32[]{:S(2)}) %all-to-all-start.1) | async-done | bytes 3145760 | tf_op jit(solution)/shard_map/all_to_all | solution.py:30
  113.4 0.0 copy-done.2
  113.4 0.0 copy-done.3
  113.4 0.0 copy-start.1
  113.4 1.2 %copy-done.1 = bf16[128,4096]{1,0:T(8,128)(2,1)S(1)} copy-done((bf16[128,4096]{1,0:T(8,128)(2,1)S(1)}, bf16[128,4096]{1,0:T(8,128)(2,1)}, u32[]{:S(2)}) %copy-start.1) | copy-done | bytes 1048600
  114.6 1.6 %shard_map.57 = f32[16,128]{1,0:T(8,128)} custom-call(s32[2,128]{1,0:T(2,128)S(1)} %bitcast.20, f32[1,128]{1,0:T(1,128)S(1)} %bitcast_convert_fusion.scales_ref, f32[16,128]{1,0:T(8,128)S(1)} %bitcast.18, bf16[128,4096]{1,0:T(8,128)(2,1)S(1)} %copy-done.1, bf16[4,384,1024]{2,1,0:T(8,128)(2,1)S(1)} %bitcast.17), custom_call_target="tpu_custom_call" | custom-call | bytes 1048576 | tf_op jit(solution)/shard_map/pallas_call | solution.py:182
  (1 shorter events, 0.0 us)
Async XLA Ops:
  33.4 5.0 %copy-start.4 = (bf16[1,128]{1,0:T(2,128)(2,1)S(1)}, bf16[1,128]{1,0:T(2,128)(2,1)}, u32[]{:S(2)}) copy-start(bf16[1,128]{1,0:T(2,128)(2,1)} %param.6) | copy-start | bytes 772
  33.4 80.0 %copy-start.2 = (f32[1,128,16]{1,2,0:T(8,128)S(1)}, f32[1,128,16]{1,2,0:T(8,128)}, u32[]{:S(2)}) copy-start(f32[1,128,16]{1,2,0:T(8,128)} %param.8) | copy-start | bytes 24580
  33.4 80.0 %copy-start.3 = (s32[1,128,2]{1,2,0:T(2,128)S(1)}, s32[1,128,2]{1,2,0:T(2,128)}, u32[]{:S(2)}) copy-start(s32[1,128,2]{1,2,0:T(2,128)} %param.7) | copy-start | bytes 3076
  33.4 80.0 %all-to-all-start.1 = ((bf16[64,24,1024]{2,1,0:T(8,128)(2,1)}), bf16[64,24,1024]{2,1,0:T(8,128)(2,1)S(1)}, u32[]{:S(2)}, u32[]{:S(2)}) async-start(bf16[64,24,1024]{2,1,0:T(8,128)(2,1)} %bitcast.21), calls=%async_computation.1 | async-start | bytes 6291456 | tf_op jit(solution)/shard_map/all_to_all | solution.py:30
  38.3 12.7 %collective-permute-start.1 = (bf16[128,4096]{1,0:T(8,128)(2,1)}, bf16[128,4096]{1,0:T(8,128)(2,1)S(1)}, u32[]{:S(2)}, u32[]{:S(2)}) collective-permute-start(bf16[128,4096]{1,0:T(8,128)(2,1)} %bitcast.23), channel_id=1, source_target_pairs={{0,448},{64,0},{128,64},{192,128},{256,192},{320,256},{384,320},{4... | collective-permute-start | bytes 3145736 | tf_op jit(solution)/shard_map/ppermute | solution.py:24
  38.3 12.6 %collective-permute-start = (bf16[128]{0:T(256)(128)(2,1)S(1)}, bf16[128]{0:T(256)(128)(2,1)S(1)}, u32[]{:S(2)}, u32[]{:S(2)}) collective-permute-start(bf16[128]{0:T(256)(128)(2,1)S(1)} %bitcast.24), channel_id=1, source_target_pairs={{0,448},{64,0},{128,64},{192,128},{256,192},{320,256},{384,320},{4... | collective-permute-start | bytes 776 | tf_op jit(solution)/shard_map/ppermute | solution.py:24
  51.0 1.0 copy-start
  113.4 1.2 %copy-start.1 = (bf16[128,4096]{1,0:T(8,128)(2,1)S(1)}, bf16[128,4096]{1,0:T(8,128)(2,1)}, u32[]{:S(2)}) copy-start(bf16[128,4096]{1,0:T(8,128)(2,1)} %copy-done) | copy-start | bytes 3145732
